TPU v7x, 256 devices: a whole 4x4x8 slice. The times are simulated.
256 devices in a mesh: row: 16 (over z, x_hi), col: 16 (over y, x_lo, core).
Axes of the slice: x: 4 (x_hi: 2, x_lo: 2; x = x_hi * 2 + x_lo), y: 4, z: 8, core: 2. Of those that a mesh axis runs over, the one named last changes fastest.
Arguments:
- schur: float32 [16, 16, 1024, 1024], P('row', 'col'), as said below
- load: float32 [16, 16, 1024, 256], P('row', 'col')
- dscale: float32 [16, 16, 1024], P('row', 'col'), may hold values from 0.3 to 3
- basis: float32 [16, 16, 8, 1024], P('row', 'col'), may hold values from -1.2 to 1.2
- coarse_inv: float32 [2048, 2048], P(('row', 'col')), as said below
- north_match: int32 [16, 16, 256], P('row', 'col'), may hold values from 0 to 255, each once within a row
- west_match: int32 [16, 16, 256], P('row', 'col'), may hold values from 0 to 255, each once within a row
Outputs:
- solution: float32 [16, 16, 1024, 256], P('row', 'col')
- residual: float32 [16, 16, 1024, 256], P('row', 'col')
Inputs may be any that keep to these rules, and one draw needn't show every extreme that they name: schur is symmetric positive definite for every subdomain. coarse_inv is symmetric positive definite. `north_match`: each row of the last dimension is a permutation of 0 to 255. `west_match`: each row of the last dimension is a permutation of 0 to 255.
All inputs are finite; a program needn't handle non-finite values.
Results may differ from a plain program's by a relative error of at most 0.0003.
Values sent between devices are 32-bit elements; how exact they have to be, the bound alone decides.
A program may use at most 128 MiB of HBM per device.

v0:
```python
import jax
import jax.numpy as jnp
from jax import lax
from jax.sharding import PartitionSpec as P

ITERS = 3


def with_halo(x, sides, width):
    for axis, dim in sides:
        size, length = (lax.axis_size(axis), x.shape[dim])
        up = [(i, (i + 1) % size) for i in range(size - 1)]
        down = [(j, i) for i, j in up]
        last = lax.slice_in_dim(x, length - width, length, axis=dim)
        first = lax.slice_in_dim(x, 0, width, axis=dim)
        before = lax.ppermute(last, axis, up)
        after = lax.ppermute(first, axis, down)
        x = jnp.concatenate([before, x, after], axis=dim)
    return x


def body(schur, load, dscale, basis, coarse_inv, north_match, west_match):
    highest = lax.Precision.HIGHEST
    face_len = north_match.shape[2]
    scenarios = load.shape[3]
    unknowns = load.shape[2]
    row_pos = lax.axis_index("row")
    col_pos = lax.axis_index("col")
    row_count = lax.axis_size("row")
    col_count = lax.axis_size("col")
    face_wt = jnp.stack(
        [
            jnp.where(row_pos > 0, 0.5, 1.0),
            jnp.where(row_pos < row_count - 1, 0.5, 1.0),
            jnp.where(col_pos > 0, 0.5, 1.0),
            jnp.where(col_pos < col_count - 1, 0.5, 1.0),
        ]
    ).astype(jnp.float32)[:, None, None]
    schur_mat = schur[0, 0]
    basis_mat = basis[0, 0]
    scale_three = dscale[0, 0].reshape(4, face_len, 1)
    north_order = north_match[0, 0]
    west_order = west_match[0, 0]

    def assemble(vec):
        north_out = jnp.zeros_like(vec[0]).at[north_order].set(vec[0])
        row_ext = with_halo(jnp.stack([north_out, vec[1]]), (("row", 0),), 1)
        north_new = vec[0] + jnp.take(row_ext[0], north_order, axis=0)
        south_new = vec[1] + row_ext[3]
        west_out = jnp.zeros_like(vec[2]).at[west_order].set(vec[2])
        col_ext = with_halo(jnp.stack([west_out, vec[3]]), (("col", 0),), 1)
        west_new = vec[2] + jnp.take(col_ext[0], west_order, axis=0)
        east_new = vec[3] + col_ext[3]
        return jnp.stack([north_new, south_new, west_new, east_new])

    def local_inner(left, right):
        return jnp.sum(face_wt * left * right, axis=(0, 1))

    def residual_sum(resid, pre_vec):
        return lax.psum(local_inner(resid, pre_vec), ("row", "col"))

    def coarse_solve(coarse_local):
        return jnp.dot(
            coarse_inv,
            lax.all_gather(coarse_local, ("row", "col"), axis=0, tiled=True),
            precision=highest,
            preferred_element_type=jnp.float32,
        )

    def precondition(vec):
        weighted = face_wt * vec
        coarse_local = jnp.dot(
            basis_mat,
            weighted.reshape(unknowns, scenarios),
            precision=highest,
            preferred_element_type=jnp.float32,
        )
        solved = coarse_solve(coarse_local)
        back = jnp.dot(basis_mat.T, solved, precision=highest, preferred_element_type=jnp.float32)
        local_part = face_wt * (scale_three * weighted + back.reshape(4, face_len, scenarios))
        return assemble(local_part)

    residual = assemble(load[0, 0].reshape(4, face_len, scenarios))
    solution = jnp.zeros_like(residual)
    pre = precondition(residual)
    direction = pre
    rz_now = residual_sum(residual, pre)
    for iteration in range(ITERS):
        product = jnp.dot(
            schur_mat,
            direction.reshape(unknowns, scenarios),
            precision=highest,
            preferred_element_type=jnp.float32,
        )
        image = assemble(product.reshape(4, face_len, scenarios))
        step_len = rz_now / lax.psum(local_inner(direction, image), ("row", "col"))
        solution = solution + step_len * direction
        residual = residual - step_len * image
        if iteration + 1 < ITERS:
            pre = precondition(residual)
            rz_next = residual_sum(residual, pre)
            direction = pre + rz_next / rz_now * direction
            rz_now = rz_next
    out_shape = (1, 1, unknowns, scenarios)
    return (solution.reshape(out_shape), residual.reshape(out_shape))


def solution(mesh):
    placed = (
        P("row", "col", None, None),
        P("row", "col", None, None),
        P("row", "col", None),
        P("row", "col", None, None),
        P(("row", "col"), None),
        P("row", "col", None),
        P("row", "col", None),
    )
    return jax.shard_map(
        body,
        mesh=mesh,
        in_specs=placed,
        out_specs=(P("row", "col", None, None), P("row", "col", None, None)),
        check_vma=False,
    )
```

profile of v0, /device:TPU:1, one launch (start us, length us, event | category | flops | bytes accessed | tf_op | source)
XLA Modules:
  0.0 2004.0 jit_solution(12698327731054816971)
XLA Ops:
  14.1 5.1 collective-permute-start.3
  21.6 5.8 collective-permute-start
  29.1 3.4 collective-permute-done
  38.0 410.9 %all-gather.4.cloned.1.call-done = f32[2048,256]{1,0:T(8,128)} async-done(((f32[8,256]{1,0:T(8,128)}), f32[2048,256]{1,0:T(8,128)}) %all-gather.4.cloned.1.call-update) | async-done | bytes 2097168 | tf_op jit(solution)/shard_map/all_gather | solution.py:65
  448.9 2.7 fusion.79
  457.3 5.0 collective-permute-start.7
  465.5 8.3 collective-permute-done.5
  475.6 3.4 collective-permute-start.4
  481.3 2.9 collective-permute-done.4
  495.4 9.1 fusion.6
  505.3 3.1 collective-permute-start.8
  508.4 3.4 collective-permute-start.10
  513.2 4.3 collective-permute-done.10
  530.0 2.7 collective-permute-start.11
  532.6 6.0 collective-permute-done.9
  544.6 79.2 %all-reduce = (f32[256]{0:T(256)S(1)}, f32[256]{0:T(256)S(1)}) all-reduce(f32[256]{0:T(256)S(1)} %get-tuple-element.4, f32[256]{0:T(256)S(1)} %get-tuple-element.3), channel_id=1, replica_groups=mesh['row'=16,'col'=16] {'row','col'}, use_global_device_ids=true, to_apply=%region_5.7 | all-reduce | flops 512 | bytes 4096 | tf_op jit(solution)/shard_map/psum | solution.py:60
  628.3 402.2 %all-gather.6.cloned.1.call-done = f32[2048,256]{1,0:T(8,128)} async-done(((f32[8,256]{1,0:T(8,128)}), f32[2048,256]{1,0:T(8,128)}) %all-gather.6.cloned.1.call-update) | async-done | bytes 2097168 | tf_op jit(solution)/shard_map/all_gather | solution.py:65
  1030.5 2.7 fusion.80
  1053.0 5.0 collective-permute-start.15
  1061.3 8.3 collective-permute-done.13
  1070.5 3.4 collective-permute-start.12
  1076.1 3.1 collective-permute-done.12
  1087.9 77.1 %psum.44 = f32[256]{0:T(256)S(1)} all-reduce(f32[256]{0:T(256)S(1)} %get-tuple-element.25), channel_id=1, replica_groups=mesh['row'=16,'col'=16] {'row','col'}, use_global_device_ids=true, to_apply=%region_13.15 | all-reduce | flops 256 | bytes 2048 | tf_op jit(solution)/shard_map/psum | solution.py:60
  1169.8 9.0 fusion.9
  1179.5 3.1 collective-permute-start.16
  1212.3 4.6 collective-permute-start.19
  1216.9 3.6 collective-permute-done.17
  1220.6 5.8 collective-permute-done.19
  1227.5 2.8 pad_maximum_fusion.4
  1230.3 74.9 %psum.45 = f32[256]{0:T(256)S(1)} all-reduce(f32[256]{0:T(256)S(1)} %get-tuple-element.11), channel_id=1, replica_groups=mesh['row'=16,'col'=16] {'row','col'}, use_global_device_ids=true, to_apply=%region_17.19 | all-reduce | flops 256 | bytes 2048 | tf_op jit(solution)/shard_map/psum | solution.py:96
  1307.6 2.5 copy.173
  1312.6 403.5 %all-gather.8.cloned.1.call-done = f32[2048,256]{1,0:T(8,128)} async-done(((f32[8,256]{1,0:T(8,128)}), f32[2048,256]{1,0:T(8,128)}) %all-gather.8.cloned.1.call-update) | async-done | bytes 2097168 | tf_op jit(solution)/shard_map/all_gather | solution.py:65
  1716.1 2.7 fusion.81
  1720.8 2.6 copy.174
  1737.7 5.0 collective-permute-start.23
  1746.0 8.3 collective-permute-done.21
  1756.2 3.4 collective-permute-start.20
  1761.7 3.1 collective-permute-done.20
  1777.8 79.7 %psum.46 = f32[256]{0:T(256)S(1)} all-reduce(f32[256]{0:T(256)S(1)} %multiply_reduce_fusion.1), channel_id=1, replica_groups=mesh['row'=16,'col'=16] {'row','col'}, use_global_device_ids=true, to_apply=%region_21.23 | all-reduce | flops 256 | bytes 2048 | tf_op jit(solution)/shard_map/psum | solution.py:60
  1857.5 2.6 multiply_add_fusion.1
  1860.4 8.7 fusion.12
  1869.2 3.1 collective-permute-start.24
  1894.9 2.6 collective-permute-start.27
  1898.8 2.6 copy.195
  1901.4 2.6 copy.172
  1912.0 2.6 copy.197
  1914.7 78.4 %psum.47 = f32[256]{0:T(256)S(1)} all-reduce(f32[256]{0:T(256)S(1)} %get-tuple-element.13), channel_id=1, replica_groups=mesh['row'=16,'col'=16] {'row','col'}, use_global_device_ids=true, to_apply=%region_25.27 | all-reduce | flops 256 | bytes 2048 | tf_op jit(solution)/shard_map/psum | solution.py:96
  1993.0 4.0 multiply_subtract_fusion
  (260 shorter events, 209.9 us)
Async XLA Ops:
  7.2 441.7 %copy-start = (f32[8,2048]{1,0:T(8,128)S(1)}, f32[8,2048]{1,0:T(8,128)}, u32[]{:S(2)}) copy-start(f32[8,2048]{1,0:T(8,128)} %param.13) | copy-start | bytes 196612
  7.2 12.1 copy-start.25
  7.2 441.7 %all-gather.4.cloned.1.call-start = ((), (), s32[]{:S(2)}) async-start(), calls=%async_computation | async-start | bytes 2105344 | tf_op jit(solution)/shard_map/all_gather | solution.py:65
  10.1 23.7 %collective-permute-start.1 = (f32[1,256,256]{1,2,0:T(8,128)S(1)}, f32[1,256,256]{1,2,0:T(8,128)S(1)}, u32[]{:S(2)}, u32[]{:S(2)}) collective-permute-start(f32[1,256,256]{1,2,0:T(8,128)S(1)} %bitcast.245), channel_id=1, source_target_pairs={{16,0},{32,16},{48,32},{64,48},{80,64},{96,80},{112,96},{128,112},... | collective-permute-start | bytes 786440 | tf_op jit(solution)/shard_map/ppermute | solution.py:17
  12.0 15.3 copy-start.33
  12.0 15.4 copy-start.34
  14.1 19.7 collective-permute-start.3
  19.5 8.4 collective-permute-start.2
  21.6 10.9 collective-permute-start
  36.6 993.9 %all-gather.6.cloned.1.call-start = ((), (), s32[]{:S(2)}) async-start(), calls=%async_computation.1 | async-start | bytes 2105344 | tf_op jit(solution)/shard_map/all_gather | solution.py:65
  457.3 8.1 collective-permute-start.7
  462.3 11.4 collective-permute-start.5
  475.6 16.5 copy-start.5
  475.6 16.5 copy-start.7
  475.6 8.7 collective-permute-start.4
  479.0 9.0 collective-permute-start.6
  505.3 6.6 collective-permute-start.8
  508.4 9.0 collective-permute-start.10
  528.7 10.0 collective-permute-start.9
  530.0 11.2 collective-permute-start.11
  627.9 1088.3 %all-gather.8.cloned.1.call-start = ((), (), s32[]{:S(2)}) async-start(), calls=%async_computation.2 | async-start | bytes 2105344 | tf_op jit(solution)/shard_map/all_gather | solution.py:65
  1039.9 30.6 %copy-start.18 = (f32[4,256,256]{1,2,0:T(8,128)}, f32[4,256,256]{1,2,0:T(8,128)S(1)}, u32[]{:S(2)}) copy-start(f32[4,256,256]{1,2,0:T(8,128)S(1)} %add_multiply_fusion.1) | copy-start | bytes 3145732
  1053.0 8.3 collective-permute-start.15
  1058.0 11.6 collective-permute-start.13
  1070.5 8.7 collective-permute-start.12
  1073.9 9.0 collective-permute-start.14
  1085.3 79.7 %copy-start.9 = (f32[1,256,256]{1,2,0:T(8,128)}, f32[1,256,256]{1,2,0:T(8,128)S(1)}, u32[]{:S(2)}) copy-start(f32[1,256,256]{1,2,0:T(8,128)S(1)} %get-tuple-element.42) | copy-start | bytes 786436
  1085.3 79.7 %copy-start.4 = (f32[1,256,256]{1,2,0:T(8,128)S(1)}, f32[1,256,256]{1,2,0:T(8,128)}, u32[]{:S(2)}) copy-start(f32[1,256,256]{1,2,0:T(8,128)} %copy-done.3) | copy-start | bytes 786436
  1085.3 79.7 %copy-start.6 = (f32[1,256,256]{1,2,0:T(8,128)S(1)}, f32[1,256,256]{1,2,0:T(8,128)}, u32[]{:S(2)}) copy-start(f32[1,256,256]{1,2,0:T(8,128)} %copy-done.5) | copy-start | bytes 786436
  1085.3 79.7 %copy-start.8 = (f32[1,256,256]{1,2,0:T(8,128)S(1)}, f32[1,256,256]{1,2,0:T(8,128)}, u32[]{:S(2)}) copy-start(f32[1,256,256]{1,2,0:T(8,128)} %copy-done.7) | copy-start | bytes 786436
  1179.5 8.0 collective-permute-start.16
  1182.6 10.2 collective-permute-start.18
  1198.8 28.7 %copy-start.10 = (f32[1,256,256]{1,2,0:T(8,128)S(1)}, f32[1,256,256]{1,2,0:T(8,128)}, u32[]{:S(2)}) copy-start(f32[1,256,256]{1,2,0:T(8,128)} %copy-done.9) | copy-start | bytes 786436
  1211.0 9.6 collective-permute-start.17
  1212.3 14.0 collective-permute-start.19
  1737.7 8.3 collective-permute-start.23
  1742.7 11.6 collective-permute-start.21
  1756.2 8.7 collective-permute-start.20
  1759.6 10.5 collective-permute-start.22
  1775.9 81.5 %copy-start.11 = (f32[1,256,256]{1,2,0:T(8,128)S(1)}, f32[1,256,256]{1,2,0:T(8,128)}, u32[]{:S(2)}) copy-start(f32[1,256,256]{1,2,0:T(8,128)} %copy-done.9) | copy-start | bytes 786436
  1869.2 8.0 collective-permute-start.24
  1872.3 8.9 collective-permute-start.26
  1882.4 15.1 copy-start.24
  1893.6 14.2 collective-permute-start.25
  1894.9 13.7 collective-permute-start.27
  1909.7 83.3 %copy-start.2 = (f32[4,256,256]{2,1,0:T(8,128)S(1)}, f32[4,256,256]{2,1,0:T(8,128)}, u32[]{:S(2)}) copy-start(f32[4,256,256]{2,1,0:T(8,128)} %copy-done.1) | copy-start | bytes 3145732
  1909.7 83.3 %copy-start.22 = (f32[4,256,256]{2,1,0:T(8,128)S(1)}, f32[4,256,256]{2,1,0:T(8,128)}, u32[]{:S(2)}) copy-start(f32[4,256,256]{2,1,0:T(8,128)} %copy.194) | copy-start | bytes 3145732
  1912.0 81.0 %copy-start.23 = (f32[4,256,256]{2,1,0:T(8,128)S(1)}, f32[4,256,256]{2,1,0:T(8,128)}, u32[]{:S(2)}) copy-start(f32[4,256,256]{2,1,0:T(8,128)} %copy.195) | copy-start | bytes 3145732
  (18 other events, 53.8 us)
Sparse Core Ops, SparseCore 0:
  36.8 412.0 all-gather.3
  628.0 402.4 all-gather.5
  1312.7 403.3 all-gather.7
where the time goes:
time: 2010 us; the launch traced here: 2000 us
  waiting for transfers between devices  1290 us (64%)
  blocking collectives  389 us (19%)
  local copies, waits for them, and re-layouts  129 us (6%)
  starting transfers between devices  81.5 us (4%)
  other arithmetic  50.6 us (3%)
  matrix products  43.7 us (2%)
    all_gather x3, waiting for transfers between devices, coarse_solve(): lax.all_gather(coarse_local, ('row', 'col'), axis=0, tiled=True)  1220 us
    psum x3, blocking collectives, residual_sum(): return lax.psum(local_inner(resid, pre_vec), ('row', 'col'))  236 us
    psum x2, blocking collectives, body(): step_len = rz_now / lax.psum(local_inner(direction, image), ('row', 'col'))  153 us
    ppermute x14, waiting for transfers between devices, with_halo(): after = lax.ppermute(first, axis, down)  48.7 us
    ppermute x14, starting transfers between devices, with_halo(): before = lax.ppermute(last, axis, up)  42 us
  transfers between devices with their start and end apart: 31, of which 24 were waited for; matrix products, arithmetic and copies ran while one was open for 2% of the time, Pallas kernels for 0%

commit v1 on v0

v1 whole, which is shorter than its diff:
```python
import functools

import jax
import jax.numpy as jnp
from jax import lax
from jax.experimental import pallas as pl
from jax.experimental.pallas import tpu as pltpu
from jax.sharding import PartitionSpec as P

MESH = pl.DeviceIdType.MESH
F = 256
NI = 1024
SC = 256
K = 8
N = 16
SB = 16
ROUNDS = 4
CHUNKS = 4
OPP = (1, 0, 3, 2)
f32, bf16 = jnp.float32, jnp.bfloat16
NT = (((1,), (1,)), ((), ()))


def mm(a, b):
    return jnp.dot(a, b, preferred_element_type=f32)


def mm_nt(a, b):
    return lax.dot_general(a, b, NT, preferred_element_type=f32)


def split(x):
    hi = x.astype(bf16)
    return hi, (x - hi.astype(f32)).astype(bf16)


def split3(x):
    hi = x.astype(bf16)
    rest = x - hi.astype(f32)
    mid = rest.astype(bf16)
    return hi, mid, (rest - mid.astype(f32)).astype(bf16)


def kernel(
    schur, load, dscale, basis, cinv, north, west,
    sol_out, res_out,
    smat, shi, slo, y, u, r, p, s, x, uhi, ulo, dcol,
    pn, pw, bds, nbr_bds, bext, bst, gst, bcat, tcat, tau, sig,
    crow, chi, clo,
    halo, p1s, p1r, ns, nr, p2s, p2r, p3s, p3r, ts, tr,
    local_sem, hs, hr, bs, br, cs, cr, s1, r1, s15, r15, s2, r2, s3, r3, s35, r35,
):
    row, col = lax.axis_index("row"), lax.axis_index("col")
    has = (row > 0, row < N - 1, col > 0, col < N - 1)
    nbr = ((row - 1, col), (row + 1, col), (row, col - 1), (row, col + 1))
    wt = [jnp.where(h, 0.5, 1.0).astype(f32) for h in has]

    get_s = pltpu.make_async_copy(schur, smat, local_sem.at[0])
    get_load = pltpu.make_async_copy(load, y, local_sem.at[1])
    get_load.start()
    get_s.start()

    barrier = pltpu.get_barrier_semaphore()

    def greet(i, _):
        pl.semaphore_signal(barrier, inc=1, device_id=(lax.rem(row + i, N), col), device_id_type=MESH)
        pl.semaphore_signal(barrier, inc=1, device_id=(row, lax.rem(col + i, N)), device_id_type=MESH)
        return 0

    lax.fori_loop(1, N, greet, 0)

    slot = lax.broadcasted_iota(jnp.int32, (F, F), 0)
    pn[...] = jnp.where(slot == north[...], 1.0, 0.0).astype(bf16)
    pw[...] = jnp.where(slot == west[...], 1.0, 0.0).astype(bf16)

    for f in range(4):

        @pl.when(jnp.logical_not(has[f]))
        def _():
            nbr_bds[f] = jnp.zeros((16, F), f32)
            for rd in range(ROUNDS):
                halo[rd, f] = jnp.zeros((F, SC), f32)
            if f < 2:
                for rd in range(ROUNDS - 1):
                    nr[rd, f] = jnp.zeros((SB, 128), f32)
                    tr[rd, f] = jnp.zeros((K, SC), f32)

    bds[0:8] = basis[...]
    bds[8:16] = jnp.where(lax.broadcasted_iota(jnp.int32, (8, NI), 0) == 0, dscale[...], 0.0)
    for f, perm in ((0, pn), (2, pw)):
        parts = split3(bds[:, f * F : (f + 1) * F])
        hi, mid, lo = [mm_nt(part, perm[...]) for part in parts]
        bds[:, f * F : (f + 1) * F] = (hi + mid) + lo

    pl.semaphore_wait(barrier, 2 * (N - 1))

    def when_each(fn, faces=(0, 1, 2, 3)):
        for f in faces:
            pl.when(has[f])(functools.partial(fn, f))

    def face_basis(f):
        return pltpu.make_async_remote_copy(
            src_ref=bds.at[:, pl.ds(f * F, F)], dst_ref=nbr_bds.at[OPP[f]], send_sem=bs.at[f], recv_sem=br.at[OPP[f]],
            device_id=nbr[f], device_id_type=MESH,
        )

    when_each(lambda f: face_basis(f).start())

    def spread(axis, src_of, dst, send_sem, recv_sem):
        def send(i, _):
            if axis == "col":
                to = lax.rem(col + i, N)
                dev = (row, to)
            else:
                to = lax.rem(row + i, N)
                dev = (to, col)
            pltpu.make_async_remote_copy(
                src_ref=src_of(to), dst_ref=dst, send_sem=send_sem, recv_sem=recv_sem, device_id=dev, device_id_type=MESH
            ).start()
            return 0

        lax.fori_loop(1, N, send, 0)

    def wait_many(buf, sem):
        part = buf.at[pl.ds(0, N - 1)]
        pltpu.make_async_copy(part, part, sem).wait()

    crow[col] = cinv[...]
    spread("col", lambda to: cinv, crow.at[col], cs.at[0], cr.at[0])

    def chunk(rd, q):
        rows = F // CHUNKS

        def one(f):
            pltpu.make_async_remote_copy(
                src_ref=y.at[pl.ds(f * F + q * rows, rows)], dst_ref=halo.at[rd, OPP[f], pl.ds(q * rows, rows)],
                send_sem=hs.at[rd, f], recv_sem=hr.at[rd, OPP[f]], device_id=nbr[f], device_id_type=MESH,
            ).start()

        when_each(one)

    def halo_sent(rd):
        def one(f):
            part = y.at[pl.ds(f * F, F)]
            pltpu.make_async_copy(part, part, hs.at[rd, f]).wait()

        when_each(one)

    def halo_wait(rd, f):
        @pl.when(has[f])
        def _():
            part = halo.at[rd, f]
            pltpu.make_async_copy(part, part, hr.at[rd, f]).wait()

    get_load.wait()
    for f, perm in ((0, pn), (2, pw)):
        parts = split3(y[f * F : (f + 1) * F, :])
        hi, mid, lo = [mm(perm[...], part) for part in parts]
        y[f * F : (f + 1) * F, :] = (hi + mid) + lo
    vhi, vlo = split(y[...])
    uhi[...] = vhi
    ulo[...] = vlo

    def wait_basis(f):
        part = nbr_bds.at[f]
        pltpu.make_async_copy(part, part, br.at[f]).wait()

    when_each(wait_basis)
    bext[...] = jnp.zeros_like(bext)
    drow = []
    for f in range(4):
        at = slice(f * F, (f + 1) * F)
        bext[0:8, at] = wt[f] * bds[0:8, at]
        bext[8 + 8 * f : 16 + 8 * f, at] = wt[f] * nbr_bds[f, 0:8]
        drow.append((wt[f] * wt[f]) * (bds[8:9, at] + nbr_bds[f, 8:9]))
    bhi, blo = split(bext[...])
    bst[0:48] = bhi
    bst[48:96] = blo

    lane = lax.broadcasted_iota(jnp.int32, (8, 128), 1)
    lane_group = lax.shift_right_logical(lane, 4)
    sub = lax.broadcasted_iota(jnp.int32, (8, 128), 0)
    lane_sq = lax.broadcasted_iota(jnp.int32, (128, 128), 1)

    def contributions(rd, mat):
        both = mm(mat[...], uhi[...])
        c48 = both[0:48] + (both[48:96] + mm(mat[0:48], ulo[...]))
        for b in range(N):
            half, at = divmod(b, 8)
            tile = jnp.zeros((8, 128), f32)
            for g in range(5):
                piece = c48[8 * g : 8 * g + 8, 128 * half : 128 * half + 128]
                shift = (16 * (g - at)) % 128
                if shift:
                    piece = pltpu.roll(piece, shift, 1)
                tile = jnp.where(lane_group == g, piece, tile)
            p1s[rd, b] = tile
        p1r[rd, col] = p1s[rd, col]
        spread("col", lambda to: p1s.at[rd, to], p1r.at[rd, col], s1.at[rd], r1.at[rd])

    def neighbour_parts(rd):
        wait_many(p1r.at[rd], r1.at[rd])
        part = p1r[rd].reshape(128, 128)
        from_east = pltpu.roll(part, 80, 1)
        from_west = pltpu.roll(part, 64, 1)
        block = part + (
            jnp.concatenate([from_east[8:], from_east[:8]], axis=0)
            + jnp.concatenate([from_west[120:], from_west[:120]], axis=0)
        )
        turned = jnp.where(lane_sq < SB, block, part).T
        ns[rd] = turned[0:48]

        def send(f):
            pltpu.make_async_remote_copy(
                src_ref=ns.at[rd, pl.ds(SB * (f + 1), SB)], dst_ref=nr.at[rd, OPP[f]], send_sem=s15.at[rd, f],
                recv_sem=r15.at[rd, OPP[f]], device_id=nbr[f], device_id_type=MESH,
            ).start()

        when_each(send, (0, 1))

    def gather_rows(rd, dots):
        def wait(f):
            part = nr.at[rd, f]
            pltpu.make_async_copy(part, part, r15.at[rd, f]).wait()

        when_each(wait, (0, 1))
        p2s[rd, 0:SB] = ns[rd, 0:SB] + (nr[rd, 0] + nr[rd, 1])
        p2s[rd, SB : SB + 8] = dots
        p2r[rd, row] = p2s[rd]
        spread("row", lambda to: p2s.at[rd], p2r.at[rd, row], s2.at[rd], r2.at[rd])

    def sum_tiles(buf, rd, at):
        total = buf[rd, 0, at : at + 8]
        for i in range(1, N):
            total = total + buf[rd, i, at : at + 8]
        return total

    def solve(rd):
        wait_many(p2r.at[rd], r2.at[rd])
        rhs = jnp.concatenate([p2r[rd, i, 0:SB] for i in range(N)], axis=1)
        hi, lo = split(rhs)
        both = mm_nt(jnp.concatenate([hi, lo], axis=0), chi[...])
        solved = both[0:SB] + (both[SB : 2 * SB] + mm_nt(hi, clo[...]))
        tiles = jnp.concatenate(
            [solved, pltpu.roll(solved, 120, 1), pltpu.roll(solved, 8, 1), jnp.zeros((80, 128), f32)], axis=0
        ).T.reshape(N, 8, 128)
        dots = sum_tiles(p2r, rd, SB)
        for i in range(N):
            p3s[rd, i, 0:8] = tiles[i]
            p3s[rd, i, 8:16] = dots
        p3r[rd, col] = p3s[rd, col]
        spread("col", lambda to: p3s.at[rd, to], p3r.at[rd, col], s3.at[rd], r3.at[rd])

    def neighbour_solutions(rd):
        wait_many(p3r.at[rd], r3.at[rd])
        out = []
        for g in range(3):
            halves = []
            for half in range(2):
                total = jnp.zeros((8, 128), f32)
                for b in range(8):
                    piece = p3r[rd, 8 * half + b, 0:8]
                    shift = (16 * (b - g)) % 128
                    if shift:
                        piece = pltpu.roll(piece, shift, 1)
                    total = jnp.where(lane_group == b, piece, total)
                halves.append(total)
            out.append(jnp.concatenate(halves, axis=1))
        ts[rd] = out[0]

        def send(f):
            pltpu.make_async_remote_copy(
                src_ref=ts.at[rd], dst_ref=tr.at[rd, OPP[f]], send_sem=s35.at[rd, f], recv_sem=r35.at[rd, OPP[f]],
                device_id=nbr[f], device_id_type=MESH,
            ).start()

        when_each(send, (0, 1))
        return out, sum_tiles(p3r, rd, 8)

    def extended_solution(rd, own):
        def wait(f):
            part = tr.at[rd, f]
            pltpu.make_async_copy(part, part, r35.at[rd, f]).wait()

        when_each(wait, (0, 1))
        return jnp.concatenate([own[0], tr[rd, 0], tr[rd, 1], own[2], own[1]], axis=0)

    def set_tau(new):
        tau[...] = new
        hi = new.astype(bf16).astype(f32)
        tcat[0:40] = hi.astype(bf16)
        tcat[64:104] = (new - hi).astype(bf16)
        tcat[128:168] = hi.astype(bf16)

    def dot_tile(delta, gamma, eps):
        tile = jnp.zeros((8, 128), f32)
        for i, v in enumerate((delta, gamma, eps)):
            if v is not None:
                tile = jnp.where(sub == 2 * i, v[:, 0:128], tile)
                tile = jnp.where(sub == 2 * i + 1, v[:, 128:256], tile)
        return tile

    def scalars(tile):
        return [jnp.concatenate([tile[2 * i : 2 * i + 1], tile[2 * i + 1 : 2 * i + 2]], axis=1) for i in range(3)]

    def prepare_rows(f):
        at = slice(f * F, (f + 1) * F)
        parts = list(split(smat[at, :]))
        for part, dst in zip(parts, (shi, slo)):
            if f == 0:
                part = mm(pn[...], part).astype(bf16)
            elif f == 2:
                part = mm(pw[...], part).astype(bf16)
            dst[at, 0:F] = mm_nt(part[:, 0:F], pn[...]).astype(bf16)
            dst[at, F : 2 * F] = part[:, F : 2 * F]
            dst[at, 2 * F : 3 * F] = mm_nt(part[:, 2 * F : 3 * F], pw[...]).astype(bf16)
            dst[at, 3 * F :] = part[:, 3 * F :]

    def new_u(f):
        at = slice(f * F, (f + 1) * F)
        d = dcol[at, :]
        res = r[at, :]
        val = jnp.concatenate([d, d], axis=1) * res + mm(bcat[at, :], tcat[...])
        u[at, :] = val
        hi, lo = split(val)
        uhi[at, :] = hi
        ulo[at, :] = lo
        return wt[f] * jnp.sum(res * val, axis=0, keepdims=True), val

    def apply_schur():
        delta = jnp.zeros((1, SC), f32)

        def block(f, total):
            at = pl.ds(pl.multiple_of(f * F, F), F)
            val = mm(shi[at, :], uhi[...]) + (mm(shi[at, :], ulo[...]) + mm(slo[at, :], uhi[...]))
            y[at, :] = val
            return total + jnp.sum(u[at, :] * val, axis=0, keepdims=True)

        return lax.fori_loop(0, 4, block, delta)

    contributions(0, bst)
    chunk(0, 0)
    get_s.wait()
    prepare_rows(0)
    prepare_rows(1)
    neighbour_parts(0)
    chunk(0, 1)
    prepare_rows(2)
    gather_rows(0, jnp.zeros((8, 128), f32))
    chunk(0, 2)
    prepare_rows(3)
    wait_many(crow, cr.at[0])
    chi_v, clo_v = split(crow[...].reshape(128, N * 128))
    chi[...] = chi_v
    clo[...] = clo_v
    solve(0)
    chunk(0, 3)
    both = mm(bst[...], shi[...])
    gt = both[0:48] + (both[48:96] + mm(bst[0:48], slo[...]))
    ghi, glo = split(gt)
    gst[0:48] = ghi
    gst[48:96] = glo
    tcat[...] = jnp.zeros_like(tcat)
    bhi32 = bext[...].astype(bf16).astype(f32)
    blo32 = bext[...] - bhi32
    pad = jnp.zeros((16, NI), f32)
    bcat[...] = jnp.concatenate([bhi32, pad, bhi32, pad, blo32, pad, jnp.zeros((64, NI), f32)], axis=0).T.astype(bf16)
    dcol[...] = jnp.broadcast_to(jnp.concatenate(drow, axis=1), (128, NI)).T
    own, _ = neighbour_solutions(0)
    set_tau(extended_solution(0, own))
    gamma = jnp.zeros((1, SC), f32)
    for f in (3, 2, 1, 0):
        at = slice(f * F, (f + 1) * F)
        halo_wait(0, f)
        r[at, :] = y[at, :] + halo[0, f]
        gamma = gamma + new_u(f)[0]
    halo_sent(0)

    eps = None
    gamma_old = pap_old = None
    for rd in range(1, ROUNDS):
        last = rd == ROUNDS - 1
        if not last:
            contributions(rd, gst)
        delta = apply_schur()
        dots = dot_tile(delta, gamma, eps)
        if not last:
            chunk(rd, 0)
            neighbour_parts(rd)
            chunk(rd, 1)
            gather_rows(rd, dots)
            chunk(rd, 2)
            solve(rd)
            chunk(rd, 3)
            own, total = neighbour_solutions(rd)
        else:
            p2s[rd, SB : SB + 8] = dots
            p2r[rd, row, SB : SB + 8] = dots
            spread("row", lambda to: p2s.at[rd, pl.ds(SB, 8)], p2r.at[rd, row, pl.ds(SB, 8)], s2.at[rd], r2.at[rd])
            for q in range(CHUNKS - 1):
                chunk(rd, q)
            wait_many(p2r.at[rd, :, pl.ds(SB, 8)], r2.at[rd])
            dots = sum_tiles(p2r, rd, SB)
            p3s[rd, 0, 8:16] = dots
            p3r[rd, col, 8:16] = dots
            spread("col", lambda to: p3s.at[rd, 0, pl.ds(8, 8)], p3r.at[rd, col, pl.ds(8, 8)], s3.at[rd], r3.at[rd])
            chunk(rd, CHUNKS - 1)
            wait_many(p3r.at[rd, :, pl.ds(8, 8)], r3.at[rd])
            total = sum_tiles(p3r, rd, 8)
        delta_t, gamma_t, eps_t = scalars(total)
        if rd == 1:
            beta = None
            pap = delta_t
        else:
            beta = gamma_t / gamma_old
            pap = delta_t + beta * (2.0 * eps_t + beta * pap_old)
        alpha = gamma_t / pap
        gamma_old, pap_old = gamma_t, pap
        if not last:
            solved = extended_solution(rd, own)
            if beta is not None:
                solved = solved + beta * sig[...]
            sig[...] = solved
            set_tau(tau[...] - alpha * solved)
        gamma = jnp.zeros((1, SC), f32)
        eps = jnp.zeros((1, SC), f32)
        for f in (3, 2, 1, 0):
            at = slice(f * F, (f + 1) * F)
            halo_wait(rd, f)
            direction = u[at, :]
            image = y[at, :] + halo[rd, f]
            if beta is not None:
                direction = direction + beta * p[at, :]
                image = image + beta * s[at, :]
            iterate = alpha * direction
            if beta is not None:
                iterate = iterate + x[at, :]
            res = r[at, :] - alpha * image
            if not last:
                x[at, :] = iterate
                r[at, :] = res
                p[at, :] = direction
                s[at, :] = image
                share, val = new_u(f)
                gamma = gamma + share
                eps = eps + wt[f] * jnp.sum(val * image, axis=0, keepdims=True)
            else:
                for val, dst in ((iterate, sol_out), (res, res_out)):
                    if f in (0, 2):
                        perm = (pn if f == 0 else pw)[...]
                        hi, mid, lo = [
                            lax.dot_general(perm, part, (((0,), (0,)), ((), ())), preferred_element_type=f32)
                            for part in split3(val)
                        ]
                        val = (hi + mid) + lo
                    dst[at, :] = val
        halo_sent(rd)

    when_each(lambda f: face_basis(f).wait_send())
    wait_many(crow, cs.at[0])
    for rd in range(ROUNDS):
        if rd < ROUNDS - 1:
            wait_many(p1r.at[rd], s1.at[rd])
            wait_many(p2r.at[rd], s2.at[rd])
            wait_many(p3r.at[rd], s3.at[rd])

            def sent(f):
                part = nr.at[rd, f]
                pltpu.make_async_copy(part, part, s15.at[rd, f]).wait()
                part = tr.at[rd, f]
                pltpu.make_async_copy(part, part, s35.at[rd, f]).wait()

            when_each(sent, (0, 1))
        else:
            wait_many(p2r.at[rd, :, pl.ds(SB, 8)], s2.at[rd])
            wait_many(p3r.at[rd, :, pl.ds(8, 8)], s3.at[rd])


def body(schur, load, dscale, basis, coarse_inv, north_match, west_match):
    vmem = pl.BlockSpec(memory_space=pltpu.VMEM)
    anywhere = pl.BlockSpec(memory_space=pl.ANY)
    dma = pltpu.SemaphoreType.DMA

    def buf(*shape, dtype=f32):
        return pltpu.VMEM(shape, dtype)

    vec = buf(NI, SC)
    half = buf(NI, SC, dtype=bf16)
    solved, left = pl.pallas_call(
        kernel,
        out_shape=[jax.ShapeDtypeStruct((NI, SC), f32)] * 2,
        in_specs=[anywhere, anywhere] + [vmem] * 5,
        out_specs=[vmem, vmem],
        scratch_shapes=[
            buf(NI, NI), buf(NI, NI, dtype=bf16), buf(NI, NI, dtype=bf16),
            vec, vec, vec, vec, vec, vec, half, half, buf(NI, 128),
            buf(F, F, dtype=bf16), buf(F, F, dtype=bf16), buf(16, NI), buf(4, 16, F), buf(48, NI),
            buf(96, NI, dtype=bf16), buf(96, NI, dtype=bf16), buf(NI, 256, dtype=bf16), buf(256, SC, dtype=bf16),
            buf(40, SC), buf(40, SC),
            buf(N, K, N * 128), buf(128, N * 128, dtype=bf16), buf(128, N * 128, dtype=bf16),
            buf(ROUNDS, 4, F, SC),
            buf(ROUNDS, N, 8, 128), buf(ROUNDS, N, 8, 128),
            buf(ROUNDS, 48, 128), buf(ROUNDS, 2, SB, 128),
            buf(ROUNDS, SB + 8, 128), buf(ROUNDS, N, SB + 8, 128),
            buf(ROUNDS, N, 16, 128), buf(ROUNDS, N, 16, 128),
            buf(ROUNDS, K, SC), buf(ROUNDS, 2, K, SC),
            dma((2,)), dma((ROUNDS, 4)), dma((ROUNDS, 4)), dma((4,)), dma((4,)), dma((1,)), dma((1,)),
            dma((ROUNDS,)), dma((ROUNDS,)), dma((ROUNDS, 2)), dma((ROUNDS, 2)), dma((ROUNDS,)), dma((ROUNDS,)),
            dma((ROUNDS,)), dma((ROUNDS,)), dma((ROUNDS, 2)), dma((ROUNDS, 2)),
        ],
        compiler_params=pltpu.CompilerParams(collective_id=0, has_side_effects=True, vmem_limit_bytes=52 << 20),
    )(
        schur.reshape(NI, NI), load.reshape(NI, SC), dscale.reshape(1, NI), basis.reshape(K, NI),
        coarse_inv, north_match.reshape(1, F), west_match.reshape(1, F),
    )
    return solved.reshape(1, 1, NI, SC), left.reshape(1, 1, NI, SC)


def solution(mesh):
    placed = (
        P("row", "col", None, None),
        P("row", "col", None, None),
        P("row", "col", None),
        P("row", "col", None, None),
        P(("row", "col"), None),
        P("row", "col", None),
        P("row", "col", None),
    )
    return jax.shard_map(
        body,
        mesh=mesh,
        in_specs=placed,
        out_specs=(P("row", "col", None, None), P("row", "col", None, None)),
        check_vma=False,
    )
```

time: 2010 us -> 143 us (0.07)
  waiting for transfers between devices: 1290 us -> 0 us
  blocking collectives: 389 us -> 0 us
  Pallas kernels: 0 us -> 135 us
  local copies, waits for them, and re-layouts: 129 us -> 6.87 us
  starting transfers between devices: 81.5 us -> 0 us
  other arithmetic: 50.6 us -> 0 us
  matrix products: 43.7 us -> 0 us
    all_gather x3 -> x0, waiting for transfers between devices: 1220 us -> none  [coarse_solve(): lax.all_gather(coarse_local, ('row', 'col'), axis=0, tiled=True)]
    psum x5 -> x0, blocking collectives: 389 us -> none  [the longest x3 236 us: residual_sum(): return lax.psum(local_inner(resid, pre_vec), ('row', 'col'))]
    pallas_call x0 -> x1, Pallas kernels: none -> 135 us  [body(): pl.pallas_call(kernel, out_shape=[jax.ShapeDtypeStruct((NI, SC), f32)] *...]
    ppermute x28 -> x0, starting transfers between devices: 81 us -> none  [the longest x14 42 us: with_halo(): before = lax.ppermute(last, axis, up)]
    ppermute x28 -> x0, waiting for transfers between devices: 77.7 us -> none  [the longest x14 48.7 us: with_halo(): after = lax.ppermute(first, axis, down)]
    dot_general x12 -> x0, matrix products: 43.7 us -> none  [the longest x3 26.8 us: body(): jnp.dot(schur_mat, direction.reshape(unknowns, scenarios), precision=high...]
    scatter x28 -> x0, local copies, waits for them, and re-layouts: 40.2 us -> none  [the longest x14 20.5 us: assemble(): west_out = jnp.zeros_like(vec[2]).at[west_order].set(vec[2])]
    gather x28 -> x0, local copies, waits for them, and re-layouts: 25.5 us -> none  [the longest x14 13.1 us: assemble(): north_new = vec[0] + jnp.take(row_ext[0], north_order, axis=0)]
  transfers between devices with their start and end apart: 31 -> 0, of which waited for: 24 -> 0; matrix products, arithmetic and copies ran while one was open for 2% -> 0% of each run, Pallas kernels for 0% -> 0%
where the time goes in v1:
time: 143 us
  Pallas kernels  135 us (94%)
  local copies, waits for them, and re-layouts  6.87 us (5%)
    pallas_call x1, Pallas kernels, body(): pl.pallas_call(kernel, out_shape=[jax.ShapeDtypeStruct((NI, SC), f32)] *...  135 us
    unnamed x12, local copies, waits for them, and re-layouts  6.87 us

profile of v1, /device:TPU:1, one launch (start us, length us, event | category | flops | bytes accessed | tf_op | source)
XLA Modules:
  0.0 143.0 jit_solution(3085394824324660081)
XLA Ops:
  0.6 0.0 copy-start
  0.6 0.8 copy-done
  1.5 0.0 copy-start.1
  1.5 0.8 copy-done.1
  2.2 0.0 copy-start.2
  2.2 0.7 copy-done.2
  2.9 0.0 copy-start.3
  2.9 0.7 copy-done.3
  3.6 0.0 copy-start.4
  3.6 0.7 copy-done.4
  4.3 135.5 %shard_map.86 = (f32[1024,256]{1,0:T(8,128)S(1)}, f32[1024,256]{1,0:T(8,128)}) custom-call(f32[1024,1024]{1,0:T(8,128)} %bitcast.13, f32[1024,256]{1,0:T(8,128)} %bitcast.15, f32[1,1024]{1,0:T(1,128)S(1)} %bitcast.10, f32[8,1024]{1,0:T(8,128)S(1)} %bitcast.9, f32[8,2048]{1,0:T(8,128)S(1)} %copy-done, s32[1,256]{1,0:T(1,128)S(1)} %bitcast.11, ...), custom_call_target="tpu_custom_call" | custom-call | tf_op jit(solution)/shard_map/pallas_call | solution.py:489
  139.8 1.0 copy.11
  140.8 2.3 %copy.12 = f32[1,1,1024,256]{3,2,1,0:T(8,128)} copy(f32[1,1,1024,256]{3,2,1,0:T(8,128)} %bitcast.14) | data formatting | bytes 2097152
Async XLA Ops:
  0.6 0.8 copy-start
  1.5 0.8 copy-start.1
  2.2 0.7 copy-start.2
  2.9 0.7 copy-start.3
  3.6 0.7 copy-start.4

commit v2 on v1

v2 whole, which is shorter than its diff:
```python
import functools

import jax
import jax.numpy as jnp
from jax import lax
from jax.experimental import pallas as pl
from jax.experimental.pallas import tpu as pltpu
from jax.sharding import PartitionSpec as P

MESH = pl.DeviceIdType.MESH
F = 256
NI = 1024
SC = 256
K = 8
N = 16
SB = 16
ROUNDS = 4
CUTS = (0, 80, 176, 256)
OPP = (1, 0, 3, 2)
f32, bf16 = jnp.float32, jnp.bfloat16
NT = (((1,), (1,)), ((), ()))


def mm(a, b):
    return jnp.dot(a, b, preferred_element_type=f32)


def mm_nt(a, b):
    return lax.dot_general(a, b, NT, preferred_element_type=f32)


def split(x):
    hi = x.astype(bf16)
    return hi, (x - hi.astype(f32)).astype(bf16)


def split3(x):
    hi = x.astype(bf16)
    rest = x - hi.astype(f32)
    mid = rest.astype(bf16)
    return hi, mid, (rest - mid.astype(f32)).astype(bf16)


def kernel(
    schur_in, load_in, dscale_in, basis_in, cinv_in, north_in, west_in,
    sol_out, res_out,
    dscale, north, west,
    smat, shi, slo, y, u, r, p, s, x, uhi, ulo, dcol,
    pn, pw, bds, nbr_bds, bext, bst, gst, bcat, tcat, tau, sig,
    crow, chi, clo,
    halo, p1s, p1r, p1ns, p1nr, p2s, p2r, p3s, p3r, p3ns, p3nr, pm,
    local_sem, hs, hr, bs, br, cs, cr, s1, r1, s2, r2, s3, r3,
):
    row, col = lax.axis_index("row"), lax.axis_index("col")
    has = (row > 0, row < N - 1, col > 0, col < N - 1)
    nbr = ((row - 1, col), (row + 1, col), (row, col - 1), (row, col + 1))
    wt = [jnp.where(h, 0.5, 1.0).astype(f32) for h in has]

    def fetch(i, src, dst):
        copy = pltpu.make_async_copy(src, dst, local_sem.at[i])
        copy.start()
        return copy

    get_small = [
        fetch(0, north_in, north), fetch(1, west_in, west), fetch(2, basis_in, bds.at[pl.ds(0, 8)]), fetch(3, dscale_in, dscale),
    ]
    get_cinv = fetch(4, cinv_in, crow.at[col])
    get_load = fetch(5, load_in, y)
    get_s = fetch(6, schur_in, smat)

    barrier = pltpu.get_barrier_semaphore()

    def greet(i, _):
        pl.semaphore_signal(barrier, inc=1, device_id=(lax.rem(row + i, N), col), device_id_type=MESH)
        for step in (0, 1, N - 1):
            other = (lax.rem(row + step, N), lax.rem(col + i, N))
            pl.semaphore_signal(barrier, inc=1, device_id=other, device_id_type=MESH)
        return 0

    lax.fori_loop(1, N, greet, 0)

    for copy in get_small:
        copy.wait()

    slot = lax.broadcasted_iota(jnp.int32, (F, F), 0)
    pn[...] = jnp.where(slot == north[...], 1.0, 0.0).astype(bf16)
    pw[...] = jnp.where(slot == west[...], 1.0, 0.0).astype(bf16)

    for f in range(4):

        @pl.when(jnp.logical_not(has[f]))
        def _():
            nbr_bds[f] = jnp.zeros((16, F), f32)
            for rd in range(ROUNDS):
                halo[rd, f] = jnp.zeros((F, SC), f32)
            if f < 2:
                for rd in range(ROUNDS - 1):
                    p1nr[rd, f] = jnp.zeros((N, 1, 128), f32)
                    p3nr[rd, f] = jnp.zeros((N, 1, 128), f32)

    bds[8:16] = jnp.where(lax.broadcasted_iota(jnp.int32, (8, NI), 0) == 0, dscale[...], 0.0)
    for f, perm in ((0, pn), (2, pw)):
        parts = split3(bds[:, f * F : (f + 1) * F])
        hi, mid, lo = [mm_nt(part, perm[...]) for part in parts]
        bds[:, f * F : (f + 1) * F] = (hi + mid) + lo

    pl.semaphore_wait(barrier, 4 * (N - 1))

    def when_each(fn, faces=(0, 1, 2, 3)):
        for f in faces:
            pl.when(has[f])(functools.partial(fn, f))

    def face_basis(f):
        return pltpu.make_async_remote_copy(
            src_ref=bds.at[:, pl.ds(f * F, F)], dst_ref=nbr_bds.at[OPP[f]], send_sem=bs.at[f], recv_sem=br.at[OPP[f]],
            device_id=nbr[f], device_id_type=MESH,
        )

    when_each(lambda f: face_basis(f).start())

    def copy_to(src, dst, send_sem, recv_sem, dev):
        return pltpu.make_async_remote_copy(
            src_ref=src, dst_ref=dst, send_sem=send_sem, recv_sem=recv_sem, device_id=dev, device_id_type=MESH
        )

    def along_col(first, up, src_of, dst, send_sem, recv_sem):
        def send(i, _):
            to = lax.rem(col + i, N)
            copy_to(src_of(to), dst, send_sem, recv_sem, (row - up, to)).start()
            return 0

        lax.fori_loop(first, N, send, 0)

    def three_rows(up_src, down_src, up_dst, down_dst, src_of, dst, send_sem, recv_sem):
        pl.when(has[0])(lambda: along_col(0, 1, lambda to: up_src.at[to], up_dst.at[col], send_sem.at[1], recv_sem.at[2]))
        pl.when(has[1])(lambda: along_col(0, -1, lambda to: down_src.at[to], down_dst.at[col], send_sem.at[2], recv_sem.at[1]))
        along_col(1, 0, src_of, dst, send_sem.at[0], recv_sem.at[0])

    def along_row(src, dst, send_sem, recv_sem):
        def send(i, _):
            copy_to(src, dst, send_sem, recv_sem, (lax.rem(row + i, N), col)).start()
            return 0

        lax.fori_loop(1, N, send, 0)

    def wait_many(buf, sem, count=N - 1):
        part = buf.at[pl.ds(0, count)]
        pltpu.make_async_copy(part, part, sem).wait()

    def three_waits(own, other, sem):
        wait_many(own, sem.at[0])
        for f in (0, 1):
            pl.when(has[f])(functools.partial(wait_many, other.at[f], sem.at[f + 1], N))

    get_cinv.wait()
    mine = crow.at[col]

    def send_cinv(i, _):
        copy_to(mine, mine, cs.at[0], cr.at[0], (row, lax.rem(col + 2 * i, N))).start()
        return 0

    lax.fori_loop(1, N // 2, send_cinv, 0)
    partner = col + 1 - 2 * lax.rem(col, 2)

    def pass_cinv():
        wait_many(crow, cr.at[0], N // 2 - 1)

        def send(i, _):
            block = crow.at[2 * i + lax.rem(col, 2)]
            copy_to(block, block, cs.at[1], cr.at[1], (row, partner)).start()
            return 0

        lax.fori_loop(0, N // 2, send, 0)

    def chunk(rd, q):
        start, rows = CUTS[q], CUTS[q + 1] - CUTS[q]

        def one(f):
            pltpu.make_async_remote_copy(
                src_ref=y.at[pl.ds(f * F + start, rows)], dst_ref=halo.at[rd, OPP[f], pl.ds(start, rows)],
                send_sem=hs.at[rd, f], recv_sem=hr.at[rd, OPP[f]], device_id=nbr[f], device_id_type=MESH,
            ).start()

        when_each(one)

    def halo_sent(rd):
        def one(f):
            part = y.at[pl.ds(f * F, F)]
            pltpu.make_async_copy(part, part, hs.at[rd, f]).wait()

        when_each(one)

    def halo_wait(rd, f):
        @pl.when(has[f])
        def _():
            part = halo.at[rd, f]
            pltpu.make_async_copy(part, part, hr.at[rd, f]).wait()

    get_load.wait()
    for f, perm in ((0, pn), (2, pw)):
        parts = split3(y[f * F : (f + 1) * F, :])
        hi, mid, lo = [mm(perm[...], part) for part in parts]
        y[f * F : (f + 1) * F, :] = (hi + mid) + lo
    vhi, vlo = split(y[...])
    uhi[...] = vhi
    ulo[...] = vlo

    def wait_basis(f):
        part = nbr_bds.at[f]
        pltpu.make_async_copy(part, part, br.at[f]).wait()

    when_each(wait_basis)
    bext[...] = jnp.zeros_like(bext)
    drow = []
    for f in range(4):
        at = slice(f * F, (f + 1) * F)
        bext[0:8, at] = wt[f] * bds[0:8, at]
        bext[8 + 8 * f : 16 + 8 * f, at] = wt[f] * nbr_bds[f, 0:8]
        drow.append((wt[f] * wt[f]) * (bds[8:9, at] + nbr_bds[f, 8:9]))
    bhi, blo = split(bext[...])
    bst[0:48] = bhi
    bst[48:96] = blo

    lane = lax.broadcasted_iota(jnp.int32, (8, 128), 1)
    lane_group = lax.shift_right_logical(lane, 4)
    sub = lax.broadcasted_iota(jnp.int32, (8, 128), 0)
    lane_group16 = lax.shift_right_logical(lax.broadcasted_iota(jnp.int32, (SB, 128), 1), 4)
    diagonal = jnp.bitwise_and(lane_group - sub, 7)

    def turn(tile):
        out = tile
        for d in range(1, 8):
            out = jnp.where(diagonal == d, pltpu.roll(pltpu.roll(tile, SB * d, 1), 8 - d, 0), out)
        return out

    def to_blocks(part):
        return jnp.concatenate([turn(part[:, 0:128]), turn(part[:, 128:256])], axis=0)

    def from_blocks(part):
        return jnp.concatenate([turn(part[0:8]), turn(part[8:16])], axis=1)

    def rows_tile(rows):
        tile = jnp.zeros((8, 128), f32)
        for i, v in enumerate(rows):
            tile = jnp.where(sub == i, v, tile)
        return tile


    def contributions(rd, mat):
        both = mm(mat[...], uhi[...])
        c48 = both[0:48] + (both[48:96] + mm(mat[0:48], ulo[...]))
        own, north_part, south_part, west_part, east_part = [to_blocks(c48[8 * g : 8 * g + 8]) for g in range(5)]
        p1ns[rd, 0] = north_part.reshape(N, 1, 128)
        p1ns[rd, 1] = south_part.reshape(N, 1, 128)
        for b in range(N):
            p1s[rd, b] = rows_tile([part[b : b + 1] for part in (own, west_part, east_part)])
        p1r[rd, col] = p1s[rd, col]
        three_rows(
            p1ns.at[rd, 0], p1ns.at[rd, 1], p1nr.at[rd, 1], p1nr.at[rd, 0], lambda to: p1s.at[rd, to], p1r.at[rd, col],
            s1.at[rd], r1.at[rd],
        )

    def up_one(a):
        return jnp.concatenate([a[1:], a[:1]], axis=0)

    def down_one(a):
        return jnp.concatenate([a[N - 1 :], a[: N - 1]], axis=0)

    def gather_rows(rd, dots):
        three_waits(p1r.at[rd], p1nr.at[rd], r1.at[rd])
        own, west_part, east_part = [
            jnp.concatenate([p1r[rd, i, g : g + 1] for i in range(N)], axis=0) for g in range(3)
        ]
        block = (own + (p1nr[rd, 0].reshape(N, 128) + p1nr[rd, 1].reshape(N, 128))) + (up_one(west_part) + down_one(east_part))
        turned = jnp.concatenate([block, jnp.zeros((128 - N, 128), f32)], axis=0).T
        rhs = turned[0:SB]
        for k in range(1, K):
            rhs = jnp.where(lane_group16 == k, pltpu.roll(turned[SB * k : SB * k + SB], SB * k, 1), rhs)
        p2s[rd, 0:SB] = rhs
        p2s[rd, SB : SB + 8] = dots
        p2r[rd, row] = p2s[rd]
        along_row(p2s.at[rd], p2r.at[rd, row], s2.at[rd], r2.at[rd])

    def sum_tiles(buf, at):
        total = buf[0, at : at + 8]
        for i in range(1, N):
            total = total + buf[i, at : at + 8]
        return total

    def solve(rd):
        wait_many(p2r.at[rd], r2.at[rd])
        rhs = jnp.concatenate([p2r[rd, i, 0:SB] for i in range(N)], axis=1)
        hi, lo = split(rhs)
        both = mm_nt(jnp.concatenate([hi, lo], axis=0), chi[...])
        solved = both[0:SB] + (both[SB : 2 * SB] + mm_nt(hi, clo[...]))
        pieces = [solved] + [pltpu.roll(solved, 128 - SB * k, 1) for k in range(1, K)]
        own = jnp.concatenate(pieces, axis=0).T[0:N]
        east_of, west_of = up_one(own), down_one(own)
        dots = sum_tiles(p2r.at[rd], SB)
        p3ns[rd] = own.reshape(N, 1, 128)
        for i in range(N):
            p3s[rd, i, 0:8] = rows_tile([part[i : i + 1] for part in (own, west_of, east_of)])
            p3s[rd, i, 8:16] = dots
        p3r[rd, col] = p3s[rd, col]
        three_rows(
            p3ns.at[rd], p3ns.at[rd], p3nr.at[rd, 1], p3nr.at[rd, 0], lambda to: p3s.at[rd, to], p3r.at[rd, col],
            s3.at[rd], r3.at[rd],
        )

    def solutions(rd):
        three_waits(p3r.at[rd], p3nr.at[rd], r3.at[rd])
        own, west_of, east_of = [jnp.concatenate([p3r[rd, i, g : g + 1] for i in range(N)], axis=0) for g in range(3)]
        parts = [own, p3nr[rd, 0].reshape(N, 128), p3nr[rd, 1].reshape(N, 128), west_of, east_of]
        return jnp.concatenate([from_blocks(part) for part in parts], axis=0), sum_tiles(p3r.at[rd], 8)

    def set_tau(new):
        tau[...] = new
        hi = new.astype(bf16).astype(f32)
        tcat[0:40] = hi.astype(bf16)
        tcat[64:104] = (new - hi).astype(bf16)
        tcat[128:168] = hi.astype(bf16)

    def dot_tile(delta, gamma, eps):
        tile = jnp.zeros((8, 128), f32)
        for i, v in enumerate((delta, gamma, eps)):
            if v is not None:
                tile = jnp.where(sub == 2 * i, v[:, 0:128], tile)
                tile = jnp.where(sub == 2 * i + 1, v[:, 128:256], tile)
        return tile

    def scalars(tile):
        return [jnp.concatenate([tile[2 * i : 2 * i + 1], tile[2 * i + 1 : 2 * i + 2]], axis=1) for i in range(3)]

    def prepare_rows(f):
        at = slice(f * F, (f + 1) * F)
        parts = list(split(smat[at, :]))
        for part, dst in zip(parts, (shi, slo)):
            if f == 0:
                part = mm(pn[...], part).astype(bf16)
            elif f == 2:
                part = mm(pw[...], part).astype(bf16)
            dst[at, 0:F] = mm_nt(part[:, 0:F], pn[...]).astype(bf16)
            dst[at, F : 2 * F] = part[:, F : 2 * F]
            dst[at, 2 * F : 3 * F] = mm_nt(part[:, 2 * F : 3 * F], pw[...]).astype(bf16)
            dst[at, 3 * F :] = part[:, 3 * F :]

    def new_u(f):
        at = slice(f * F, (f + 1) * F)
        d = dcol[at, :]
        res = r[at, :]
        val = jnp.concatenate([d, d], axis=1) * res + mm(bcat[at, :], tcat[...])
        u[at, :] = val
        hi, lo = split(val)
        uhi[at, :] = hi
        ulo[at, :] = lo
        return wt[f] * jnp.sum(res * val, axis=0, keepdims=True), val

    def own_order(f, val):
        if f in (1, 3):
            return val
        perm = (pn if f == 0 else pw)[...]
        hi, mid, lo = [
            lax.dot_general(perm, part, (((0,), (0,)), ((), ())), preferred_element_type=f32) for part in split3(val)
        ]
        return (hi + mid) + lo

    def apply_schur():
        delta = jnp.zeros((1, SC), f32)

        def block(f, total):
            at = pl.ds(pl.multiple_of(f * F, F), F)
            val = mm(shi[at, :], uhi[...]) + (mm(shi[at, :], ulo[...]) + mm(slo[at, :], uhi[...]))
            y[at, :] = val
            return total + jnp.sum(u[at, :] * val, axis=0, keepdims=True)

        return lax.fori_loop(0, 4, block, delta)

    contributions(0, bst)
    chunk(0, 0)
    get_s.wait()
    prepare_rows(0)
    prepare_rows(1)
    gather_rows(0, jnp.zeros((8, 128), f32))
    pass_cinv()
    chunk(0, 1)
    prepare_rows(2)
    prepare_rows(3)
    wait_many(crow, cr.at[1], N // 2)
    order = lax.broadcasted_iota(jnp.int32, (128, 128), 0)
    order = jnp.bitwise_and(order, N - 1) * K + lax.shift_right_logical(order, 4)
    pm[...] = jnp.where(order == lax.broadcasted_iota(jnp.int32, (128, 128), 1), 1.0, 0.0).astype(bf16)
    for part, dst in zip(split(crow[...].reshape(128, N * 128)), (chi, clo)):
        part = mm(pm[...], part).astype(bf16)
        for i in range(N):
            dst[:, i * 128 : i * 128 + 128] = mm_nt(part[:, i * 128 : i * 128 + 128], pm[...]).astype(bf16)
    solve(0)
    chunk(0, 2)
    both = mm(bst[...], shi[...])
    gt = both[0:48] + (both[48:96] + mm(bst[0:48], slo[...]))
    ghi, glo = split(gt)
    gst[0:48] = ghi
    gst[48:96] = glo
    tcat[...] = jnp.zeros_like(tcat)
    bhi32 = bext[...].astype(bf16).astype(f32)
    blo32 = bext[...] - bhi32
    pad = jnp.zeros((16, NI), f32)
    bcat[...] = jnp.concatenate([bhi32, pad, bhi32, pad, blo32, pad, jnp.zeros((64, NI), f32)], axis=0).T.astype(bf16)
    dcol[...] = jnp.broadcast_to(jnp.concatenate(drow, axis=1), (128, NI)).T
    set_tau(solutions(0)[0])
    gamma = jnp.zeros((1, SC), f32)
    for f in (3, 2, 1, 0):
        at = slice(f * F, (f + 1) * F)
        halo_wait(0, f)
        r[at, :] = y[at, :] + halo[0, f]
        gamma = gamma + new_u(f)[0]
    halo_sent(0)

    eps = None
    gamma_old = pap_old = None
    for rd in range(1, ROUNDS):
        last = rd == ROUNDS - 1
        if not last:
            contributions(rd, gst)
        delta = apply_schur()
        dots = dot_tile(delta, gamma, eps)
        if not last:
            chunk(rd, 0)
            gather_rows(rd, dots)
            chunk(rd, 1)
            solve(rd)
            chunk(rd, 2)
            solved, total = solutions(rd)
        else:
            p2s[rd, SB : SB + 8] = dots
            p2r[rd, row, SB : SB + 8] = dots
            along_row(p2s.at[rd, pl.ds(SB, 8)], p2r.at[rd, row, pl.ds(SB, 8)], s2.at[rd], r2.at[rd])
            chunk(rd, 0)
            chunk(rd, 1)
            wait_many(p2r.at[rd, :, pl.ds(SB, 8)], r2.at[rd])
            dots = sum_tiles(p2r.at[rd], SB)
            p3s[rd, 0, 8:16] = dots
            p3r[rd, col, 8:16] = dots
            along_col(1, 0, lambda to: p3s.at[rd, 0, pl.ds(8, 8)], p3r.at[rd, col, pl.ds(8, 8)], s3.at[rd, 0], r3.at[rd, 0])
            chunk(rd, 2)
            wait_many(p3r.at[rd, :, pl.ds(8, 8)], r3.at[rd, 0])
            total = sum_tiles(p3r.at[rd], 8)
        delta_t, gamma_t, eps_t = scalars(total)
        if rd == 1:
            beta = None
            pap = delta_t
        else:
            beta = gamma_t / gamma_old
            pap = delta_t + beta * (2.0 * eps_t + beta * pap_old)
        alpha = gamma_t / pap
        gamma_old, pap_old = gamma_t, pap
        if not last:
            if beta is not None:
                solved = solved + beta * sig[...]
            sig[...] = solved
            set_tau(tau[...] - alpha * solved)
        for f in range(4):
            at = slice(f * F, (f + 1) * F)
            direction = u[at, :]
            if beta is not None:
                direction = direction + beta * p[at, :]
            iterate = alpha * direction
            if beta is not None:
                iterate = iterate + x[at, :]
            if last:
                sol_out[at, :] = own_order(f, iterate)
            else:
                p[at, :] = direction
                x[at, :] = iterate
        gamma = jnp.zeros((1, SC), f32)
        eps = jnp.zeros((1, SC), f32)
        for f in (3, 2, 1, 0):
            at = slice(f * F, (f + 1) * F)
            halo_wait(rd, f)
            image = y[at, :] + halo[rd, f]
            if beta is not None:
                image = image + beta * s[at, :]
            res = r[at, :] - alpha * image
            if last:
                res_out[at, :] = own_order(f, res)
            else:
                r[at, :] = res
                s[at, :] = image
                share, val = new_u(f)
                gamma = gamma + share
                eps = eps + wt[f] * jnp.sum(val * image, axis=0, keepdims=True)
        halo_sent(rd)

    when_each(lambda f: face_basis(f).wait_send())
    wait_many(crow, cs.at[0], N // 2 - 1)
    wait_many(crow, cs.at[1], N // 2)
    for rd in range(ROUNDS):
        if rd < ROUNDS - 1:
            three_waits(p1r.at[rd], p1nr.at[rd], s1.at[rd])
            wait_many(p2r.at[rd], s2.at[rd])
            three_waits(p3r.at[rd], p3nr.at[rd], s3.at[rd])
        else:
            wait_many(p2r.at[rd, :, pl.ds(SB, 8)], s2.at[rd])
            wait_many(p3r.at[rd, :, pl.ds(8, 8)], s3.at[rd, 0])


def body(schur, load, dscale, basis, coarse_inv, north_match, west_match):
    vmem = pl.BlockSpec(memory_space=pltpu.VMEM)
    hbm = pl.BlockSpec(memory_space=pltpu.HBM)
    dma = pltpu.SemaphoreType.DMA

    def buf(*shape, dtype=f32):
        return pltpu.VMEM(shape, dtype)

    vec = buf(NI, SC)
    half = buf(NI, SC, dtype=bf16)
    solved, left = pl.pallas_call(
        kernel,
        out_shape=[jax.ShapeDtypeStruct((NI, SC), f32)] * 2,
        in_specs=[hbm] * 7,
        out_specs=[vmem, vmem],
        scratch_shapes=[
            buf(1, NI), buf(1, F, dtype=jnp.int32), buf(1, F, dtype=jnp.int32),
            buf(NI, NI), buf(NI, NI, dtype=bf16), buf(NI, NI, dtype=bf16),
            vec, vec, vec, vec, vec, vec, half, half, buf(NI, 128),
            buf(F, F, dtype=bf16), buf(F, F, dtype=bf16), buf(16, NI), buf(4, 16, F), buf(48, NI),
            buf(96, NI, dtype=bf16), buf(96, NI, dtype=bf16), buf(NI, 256, dtype=bf16), buf(256, SC, dtype=bf16),
            buf(40, SC), buf(40, SC),
            buf(N, K, N * 128), buf(128, N * 128, dtype=bf16), buf(128, N * 128, dtype=bf16),
            buf(ROUNDS, 4, F, SC),
            buf(ROUNDS, N, 8, 128), buf(ROUNDS, N, 8, 128), buf(ROUNDS, 2, N, 1, 128), buf(ROUNDS, 2, N, 1, 128),
            buf(ROUNDS, SB + 8, 128), buf(ROUNDS, N, SB + 8, 128),
            buf(ROUNDS, N, 16, 128), buf(ROUNDS, N, 16, 128), buf(ROUNDS, N, 1, 128), buf(ROUNDS, 2, N, 1, 128),
            buf(128, 128, dtype=bf16),
            dma((7,)), dma((ROUNDS, 4)), dma((ROUNDS, 4)), dma((4,)), dma((4,)), dma((2,)), dma((2,)),
            dma((ROUNDS, 3)), dma((ROUNDS, 3)), dma((ROUNDS,)), dma((ROUNDS,)), dma((ROUNDS, 3)), dma((ROUNDS, 3)),
        ],
        compiler_params=pltpu.CompilerParams(collective_id=0, has_side_effects=True, vmem_limit_bytes=52 << 20),
    )(
        schur.reshape(NI, NI), load.reshape(NI, SC), dscale.reshape(1, NI), basis.reshape(K, NI),
        coarse_inv, north_match.reshape(1, F), west_match.reshape(1, F),
    )
    return solved.reshape(1, 1, NI, SC), left.reshape(1, 1, NI, SC)


def solution(mesh):
    placed = (
        P("row", "col", None, None),
        P("row", "col", None, None),
        P("row", "col", None),
        P("row", "col", None, None),
        P(("row", "col"), None),
        P("row", "col", None),
        P("row", "col", None),
    )
    return jax.shard_map(
        body,
        mesh=mesh,
        in_specs=placed,
        out_specs=(P("row", "col", None, None), P("row", "col", None, None)),
        check_vma=False,
    )
```

time: 143 us -> 128 us (0.90)
  Pallas kernels: 135 us -> 120 us
    pallas_call x1, Pallas kernels: 135 us -> 120 us  [body(): pl.pallas_call(kernel, out_shape=[jax.ShapeDtypeStruct((NI, SC), f32)] *...]
where the time goes in v2:
time: 128 us; the launch traced here: 127 us
  Pallas kernels  120 us (94%)
  local copies, waits for them, and re-layouts  6.87 us (5%)
    pallas_call x1, Pallas kernels, body(): pl.pallas_call(kernel, out_shape=[jax.ShapeDtypeStruct((NI, SC), f32)] *...  120 us
    unnamed x12, local copies, waits for them, and re-layouts  6.87 us

profile of v2, /device:TPU:1, one launch (start us, length us, event | category | flops | bytes accessed | tf_op | source)
XLA Modules:
  0.0 127.2 jit_solution(302000773116272219)
XLA Ops:
  0.6 0.0 copy-start
  0.6 0.8 copy-done
  1.5 0.0 copy-start.1
  1.5 0.8 copy-done.1
  2.2 0.0 copy-start.2
  2.2 0.7 copy-done.2
  2.9 0.0 copy-start.3
  2.9 0.7 copy-done.3
  3.6 0.0 copy-start.4
  3.6 0.7 copy-done.4
  4.3 119.7 %shard_map.86 = (f32[1024,256]{1,0:T(8,128)S(1)}, f32[1024,256]{1,0:T(8,128)}) custom-call(f32[1024,1024]{1,0:T(8,128)} %bitcast.13, f32[1024,256]{1,0:T(8,128)} %bitcast.15, f32[1,1024]{1,0:T(1,128)S(1)} %bitcast.10, f32[8,1024]{1,0:T(8,128)S(1)} %bitcast.9, f32[8,2048]{1,0:T(8,128)S(1)} %copy-done, s32[1,256]{1,0:T(1,128)S(1)} %bitcast.11, ...), custom_call_target="tpu_custom_call" | custom-call | tf_op jit(solution)/shard_map/pallas_call | solution.py:516
  124.0 1.0 copy.11
  125.0 2.3 %copy.12 = f32[1,1,1024,256]{3,2,1,0:T(8,128)} copy(f32[1,1,1024,256]{3,2,1,0:T(8,128)} %bitcast.14) | data formatting | bytes 2097152
Async XLA Ops:
  0.6 0.8 copy-start
  1.5 0.8 copy-start.1
  2.2 0.7 copy-start.2
  2.9 0.7 copy-start.3
  3.6 0.7 copy-start.4

commit v3 on v2

--- a/solution.py
+++ b/solution.py
@@ -15,7 +15,7 @@
 N = 16
 SB = 16
 ROUNDS = 4
-CUTS = (0, 80, 176, 256)
+CUTS = ((0, 0, 96, 96, 192, 256), (0, 96, 96, 192, 256), (0, 96, 96, 192, 256), (0, 96, 160, 208, 256))
 OPP = (1, 0, 3, 2)
 f32, bf16 = jnp.float32, jnp.bfloat16
 NT = (((1,), (1,)), ((), ()))
@@ -45,11 +45,11 @@
     schur_in, load_in, dscale_in, basis_in, cinv_in, north_in, west_in,
     sol_out, res_out,
     dscale, north, west,
-    smat, shi, slo, y, u, r, p, s, x, uhi, ulo, dcol,
+    smat, shi, slo, y, us, r, p, s, x, uhi, ulo, dcol,
     pn, pw, bds, nbr_bds, bext, bst, gst, bcat, tcat, tau, sig,
     crow, chi, clo,
     halo, p1s, p1r, p1ns, p1nr, p2s, p2r, p3s, p3r, p3ns, p3nr, pm,
-    local_sem, hs, hr, bs, br, cs, cr, s1, r1, s2, r2, s3, r3,
+    local_sem, hs, hr, bs, br, cs, cr, s1, r1, s2, r2, s3, r3, out_sem,
 ):
     row, col = lax.axis_index("row"), lax.axis_index("col")
     has = (row > 0, row < N - 1, col > 0, col < N - 1)
@@ -77,7 +77,7 @@
             pl.semaphore_signal(barrier, inc=1, device_id=other, device_id_type=MESH)
         return 0
 
-    lax.fori_loop(1, N, greet, 0)
+    lax.fori_loop(1, N, greet, 0, unroll=True)
 
     for copy in get_small:
         copy.wait()
@@ -129,7 +129,7 @@
             copy_to(src_of(to), dst, send_sem, recv_sem, (row - up, to)).start()
             return 0
 
-        lax.fori_loop(first, N, send, 0)
+        lax.fori_loop(first, N, send, 0, unroll=True)
 
     def three_rows(up_src, down_src, up_dst, down_dst, src_of, dst, send_sem, recv_sem):
         pl.when(has[0])(lambda: along_col(0, 1, lambda to: up_src.at[to], up_dst.at[col], send_sem.at[1], recv_sem.at[2]))
@@ -141,14 +141,16 @@
             copy_to(src, dst, send_sem, recv_sem, (lax.rem(row + i, N), col)).start()
             return 0
 
-        lax.fori_loop(1, N, send, 0)
+        lax.fori_loop(1, N, send, 0, unroll=True)
 
     def wait_many(buf, sem, count=N - 1):
         part = buf.at[pl.ds(0, count)]
         pltpu.make_async_copy(part, part, sem).wait()
 
-    def three_waits(own, other, sem):
+    def three_waits(own, other, sem, between=None):
         wait_many(own, sem.at[0])
+        if between is not None:
+            between()
         for f in (0, 1):
             pl.when(has[f])(functools.partial(wait_many, other.at[f], sem.at[f + 1], N))
 
@@ -172,8 +174,11 @@
 
         lax.fori_loop(0, N // 2, send, 0)
 
-    def chunk(rd, q):
-        start, rows = CUTS[q], CUTS[q + 1] - CUTS[q]
+    def chunk(rd, q, faces=(0, 1, 2, 3)):
+        cuts = CUTS[rd]
+        start, rows = cuts[q], cuts[q + 1] - cuts[q]
+        if rows == 0:
+            return
 
         def one(f):
             pltpu.make_async_remote_copy(
@@ -181,7 +186,7 @@
                 send_sem=hs.at[rd, f], recv_sem=hr.at[rd, OPP[f]], device_id=nbr[f], device_id_type=MESH,
             ).start()
 
-        when_each(one)
+        when_each(one, faces)
 
     def halo_sent(rd):
         def one(f):
@@ -204,6 +209,8 @@
     vhi, vlo = split(y[...])
     uhi[...] = vhi
     ulo[...] = vlo
+
+    chunk(0, 0)
 
     def wait_basis(f):
         part = nbr_bds.at[f]
@@ -266,8 +273,8 @@
     def down_one(a):
         return jnp.concatenate([a[N - 1 :], a[: N - 1]], axis=0)
 
-    def gather_rows(rd, dots):
-        three_waits(p1r.at[rd], p1nr.at[rd], r1.at[rd])
+    def gather_rows(rd, dots, between):
+        three_waits(p1r.at[rd], p1nr.at[rd], r1.at[rd], between)
         own, west_part, east_part = [
             jnp.concatenate([p1r[rd, i, g : g + 1] for i in range(N)], axis=0) for g in range(3)
         ]
@@ -344,12 +351,12 @@
             dst[at, 2 * F : 3 * F] = mm_nt(part[:, 2 * F : 3 * F], pw[...]).astype(bf16)
             dst[at, 3 * F :] = part[:, 3 * F :]
 
-    def new_u(f):
+    def new_u(rd, f):
         at = slice(f * F, (f + 1) * F)
         d = dcol[at, :]
         res = r[at, :]
         val = jnp.concatenate([d, d], axis=1) * res + mm(bcat[at, :], tcat[...])
-        u[at, :] = val
+        us[(rd + 1) % 2, at, :] = val
         hi, lo = split(val)
         uhi[at, :] = hi
         ulo[at, :] = lo
@@ -364,25 +371,39 @@
         ]
         return (hi + mid) + lo
 
-    def apply_schur():
-        delta = jnp.zeros((1, SC), f32)
-
-        def block(f, total):
-            at = pl.ds(pl.multiple_of(f * F, F), F)
+    def apply_schur(rd, after_face):
+        total = jnp.zeros((1, SC), f32)
+        for f in range(4):
+            at = slice(f * F, (f + 1) * F)
             val = mm(shi[at, :], uhi[...]) + (mm(shi[at, :], ulo[...]) + mm(slo[at, :], uhi[...]))
             y[at, :] = val
-            return total + jnp.sum(u[at, :] * val, axis=0, keepdims=True)
-
-        return lax.fori_loop(0, 4, block, delta)
+            after_face(f)
+            total = total + jnp.sum(us[rd % 2, at, :] * val, axis=0, keepdims=True)
+        return total
+
+    def move(rd, alpha, beta, write):
+        for f in range(4):
+            at = slice(f * F, (f + 1) * F)
+            direction = us[rd % 2, at, :]
+            if beta is not None:
+                direction = direction + beta * p[at, :]
+            iterate = alpha * direction
+            if beta is not None:
+                iterate = iterate + x[at, :]
+            if write is None:
+                p[at, :] = direction
+                x[at, :] = iterate
+            else:
+                write(f, iterate)
 
     contributions(0, bst)
-    chunk(0, 0)
+    chunk(0, 1)
     get_s.wait()
     prepare_rows(0)
     prepare_rows(1)
-    gather_rows(0, jnp.zeros((8, 128), f32))
+    gather_rows(0, jnp.zeros((8, 128), f32), lambda: chunk(0, 2))
     pass_cinv()
-    chunk(0, 1)
+    chunk(0, 3)
     prepare_rows(2)
     prepare_rows(3)
     wait_many(crow, cr.at[1], N // 2)
@@ -394,7 +415,7 @@
         for i in range(N):
             dst[:, i * 128 : i * 128 + 128] = mm_nt(part[:, i * 128 : i * 128 + 128], pm[...]).astype(bf16)
     solve(0)
-    chunk(0, 2)
+    chunk(0, 4)
     both = mm(bst[...], shi[...])
     gt = both[0:48] + (both[48:96] + mm(bst[0:48], slo[...]))
     ghi, glo = split(gt)
@@ -412,23 +433,24 @@
         at = slice(f * F, (f + 1) * F)
         halo_wait(0, f)
         r[at, :] = y[at, :] + halo[0, f]
-        gamma = gamma + new_u(f)[0]
+        gamma = gamma + new_u(0, f)[0]
     halo_sent(0)
 
     eps = None
-    gamma_old = pap_old = None
+    gamma_old = pap_old = pending = None
     for rd in range(1, ROUNDS):
         last = rd == ROUNDS - 1
         if not last:
             contributions(rd, gst)
-        delta = apply_schur()
+        delta = apply_schur(rd, (lambda f: None) if last else (lambda f: chunk(rd, 0, (f,))))
         dots = dot_tile(delta, gamma, eps)
         if not last:
-            chunk(rd, 0)
-            gather_rows(rd, dots)
-            chunk(rd, 1)
+            if pending is not None:
+                move(*pending, None)
+            gather_rows(rd, dots, lambda: chunk(rd, 1))
+            chunk(rd, 2)
             solve(rd)
-            chunk(rd, 2)
+            chunk(rd, 3)
             solved, total = solutions(rd)
         else:
             p2s[rd, SB : SB + 8] = dots
@@ -436,12 +458,14 @@
             along_row(p2s.at[rd, pl.ds(SB, 8)], p2r.at[rd, row, pl.ds(SB, 8)], s2.at[rd], r2.at[rd])
             chunk(rd, 0)
             chunk(rd, 1)
+            chunk(rd, 2)
+            move(*pending, None)
             wait_many(p2r.at[rd, :, pl.ds(SB, 8)], r2.at[rd])
             dots = sum_tiles(p2r.at[rd], SB)
             p3s[rd, 0, 8:16] = dots
             p3r[rd, col, 8:16] = dots
             along_col(1, 0, lambda to: p3s.at[rd, 0, pl.ds(8, 8)], p3r.at[rd, col, pl.ds(8, 8)], s3.at[rd, 0], r3.at[rd, 0])
-            chunk(rd, 2)
+            chunk(rd, 3)
             wait_many(p3r.at[rd, :, pl.ds(8, 8)], r3.at[rd, 0])
             total = sum_tiles(p3r.at[rd], 8)
         delta_t, gamma_t, eps_t = scalars(total)
@@ -458,19 +482,14 @@
                 solved = solved + beta * sig[...]
             sig[...] = solved
             set_tau(tau[...] - alpha * solved)
-        for f in range(4):
-            at = slice(f * F, (f + 1) * F)
-            direction = u[at, :]
-            if beta is not None:
-                direction = direction + beta * p[at, :]
-            iterate = alpha * direction
-            if beta is not None:
-                iterate = iterate + x[at, :]
-            if last:
-                sol_out[at, :] = own_order(f, iterate)
-            else:
-                p[at, :] = direction
-                x[at, :] = iterate
+        if last:
+
+            def write(f, val):
+                x[f * F : (f + 1) * F, :] = own_order(f, val)
+                pltpu.make_async_copy(x.at[pl.ds(f * F, F)], sol_out.at[pl.ds(f * F, F)], out_sem.at[0]).start()
+
+            move(rd, alpha, beta, write)
+        pending = (rd, alpha, beta)
         gamma = jnp.zeros((1, SC), f32)
         eps = jnp.zeros((1, SC), f32)
         for f in (3, 2, 1, 0):
@@ -481,15 +500,18 @@
                 image = image + beta * s[at, :]
             res = r[at, :] - alpha * image
             if last:
-                res_out[at, :] = own_order(f, res)
+                r[at, :] = own_order(f, res)
+                pltpu.make_async_copy(r.at[pl.ds(f * F, F)], res_out.at[pl.ds(f * F, F)], out_sem.at[1]).start()
             else:
                 r[at, :] = res
                 s[at, :] = image
-                share, val = new_u(f)
+                share, val = new_u(rd, f)
                 gamma = gamma + share
                 eps = eps + wt[f] * jnp.sum(val * image, axis=0, keepdims=True)
         halo_sent(rd)
 
+    pltpu.make_async_copy(x, sol_out, out_sem.at[0]).wait()
+    pltpu.make_async_copy(r, res_out, out_sem.at[1]).wait()
     when_each(lambda f: face_basis(f).wait_send())
     wait_many(crow, cs.at[0], N // 2 - 1)
     wait_many(crow, cs.at[1], N // 2)
@@ -517,11 +539,11 @@
         kernel,
         out_shape=[jax.ShapeDtypeStruct((NI, SC), f32)] * 2,
         in_specs=[hbm] * 7,
-        out_specs=[vmem, vmem],
+        out_specs=[hbm, hbm],
         scratch_shapes=[
             buf(1, NI), buf(1, F, dtype=jnp.int32), buf(1, F, dtype=jnp.int32),
             buf(NI, NI), buf(NI, NI, dtype=bf16), buf(NI, NI, dtype=bf16),
-            vec, vec, vec, vec, vec, vec, half, half, buf(NI, 128),
+            vec, buf(2, NI, SC), vec, vec, vec, vec, half, half, buf(NI, 128),
             buf(F, F, dtype=bf16), buf(F, F, dtype=bf16), buf(16, NI), buf(4, 16, F), buf(48, NI),
             buf(96, NI, dtype=bf16), buf(96, NI, dtype=bf16), buf(NI, 256, dtype=bf16), buf(256, SC, dtype=bf16),
             buf(40, SC), buf(40, SC),
@@ -532,9 +554,9 @@
             buf(ROUNDS, N, 16, 128), buf(ROUNDS, N, 16, 128), buf(ROUNDS, N, 1, 128), buf(ROUNDS, 2, N, 1, 128),
             buf(128, 128, dtype=bf16),
             dma((7,)), dma((ROUNDS, 4)), dma((ROUNDS, 4)), dma((4,)), dma((4,)), dma((2,)), dma((2,)),
-            dma((ROUNDS, 3)), dma((ROUNDS, 3)), dma((ROUNDS,)), dma((ROUNDS,)), dma((ROUNDS, 3)), dma((ROUNDS, 3)),
+            dma((ROUNDS, 3)), dma((ROUNDS, 3)), dma((ROUNDS,)), dma((ROUNDS,)), dma((ROUNDS, 3)), dma((ROUNDS, 3)), dma((2,)),
         ],
-        compiler_params=pltpu.CompilerParams(collective_id=0, has_side_effects=True, vmem_limit_bytes=52 << 20),
+        compiler_params=pltpu.CompilerParams(collective_id=0, has_side_effects=True, vmem_limit_bytes=63 << 20),
     )(
         schur.reshape(NI, NI), load.reshape(NI, SC), dscale.reshape(1, NI), basis.reshape(K, NI),
         coarse_inv, north_match.reshape(1, F), west_match.reshape(1, F),

time: 128 us -> 123 us (0.961)
  local copies, waits for them, and re-layouts: 6.87 us -> 4.52 us
  Pallas kernels: 120 us -> 118 us
    unnamed x12 -> x2, local copies, waits for them, and re-layouts: 6.87 us -> 4.52 us
    pallas_call x1, Pallas kernels: 120 us -> 118 us  [body(): pl.pallas_call(kernel, out_shape=[jax.ShapeDtypeStruct((NI, SC), f32)] *...]
where the time goes in v3:
time: 123 us
  Pallas kernels  118 us (96%)
  local copies, waits for them, and re-layouts  4.52 us (4%)
    pallas_call x1, Pallas kernels, body(): pl.pallas_call(kernel, out_shape=[jax.ShapeDtypeStruct((NI, SC), f32)] *...  118 us
    unnamed x2, local copies, waits for them, and re-layouts  4.52 us

profile of v3, /device:TPU:1, one launch (start us, length us, event | category | flops | bytes accessed | tf_op | source)
XLA Modules:
  0.0 123.2 jit_solution(12907836614477089130)
XLA Ops:
  0.6 118.1 %shard_map.86 = (f32[1024,256]{1,0:T(8,128)}, f32[1024,256]{1,0:T(8,128)}) custom-call(f32[1024,1024]{1,0:T(8,128)} %bitcast.8, f32[1024,256]{1,0:T(8,128)} %bitcast.11, f32[1,1024]{1,0:T(1,128)} %bitcast.13, f32[8,1024]{1,0:T(8,128)} %bitcast.12, f32[8,2048]{1,0:T(8,128)} %cinv_in.1, s32[1,256]{1,0:T(1,128)} %bitcast.14, s32[1,256]{1,0:T(1,128)} %bitcast.15), custom_call_target="tpu_custom_call" | custom-call | tf_op jit(solution)/shard_map/pallas_call | solution.py:538
  118.7 2.3 %copy.11 = f32[1,1,1024,256]{3,2,1,0:T(8,128)} copy(f32[1,1,1024,256]{3,2,1,0:T(8,128)} %bitcast.10) | data formatting | bytes 2097152
  121.0 2.3 %copy.12 = f32[1,1,1024,256]{3,2,1,0:T(8,128)} copy(f32[1,1,1024,256]{3,2,1,0:T(8,128)} %bitcast.9) | data formatting | bytes 2097152

commit v4 on v3

--- a/solution.py
+++ b/solution.py
@@ -16,6 +16,7 @@
 SB = 16
 ROUNDS = 4
 CUTS = ((0, 0, 96, 96, 192, 256), (0, 96, 96, 192, 256), (0, 96, 96, 192, 256), (0, 96, 160, 208, 256))
+PIECES = 4
 OPP = (1, 0, 3, 2)
 f32, bf16 = jnp.float32, jnp.bfloat16
 NT = (((1,), (1,)), ((), ()))
@@ -48,8 +49,8 @@
     smat, shi, slo, y, us, r, p, s, x, uhi, ulo, dcol,
     pn, pw, bds, nbr_bds, bext, bst, gst, bcat, tcat, tau, sig,
     crow, chi, clo,
-    halo, p1s, p1r, p1ns, p1nr, p2s, p2r, p3s, p3r, p3ns, p3nr, pm,
-    local_sem, hs, hr, bs, br, cs, cr, s1, r1, s2, r2, s3, r3, out_sem,
+    halo, p1s, p1r, p1ns, p1nr, p2s, p2r, p3s, p3r, p3ns, p3nr, pm, d2s, d2r, d3s, d3r,
+    local_sem, hs, hr, bs, br, cs, cr, s1, r1, s2, r2, s3, r3, out_sem, s4, r4, s5, r5,
 ):
     row, col = lax.axis_index("row"), lax.axis_index("col")
     has = (row > 0, row < N - 1, col > 0, col < N - 1)
@@ -273,7 +274,7 @@
     def down_one(a):
         return jnp.concatenate([a[N - 1 :], a[: N - 1]], axis=0)
 
-    def gather_rows(rd, dots, between):
+    def gather_rows(rd, between):
         three_waits(p1r.at[rd], p1nr.at[rd], r1.at[rd], between)
         own, west_part, east_part = [
             jnp.concatenate([p1r[rd, i, g : g + 1] for i in range(N)], axis=0) for g in range(3)
@@ -283,31 +284,44 @@
         rhs = turned[0:SB]
         for k in range(1, K):
             rhs = jnp.where(lane_group16 == k, pltpu.roll(turned[SB * k : SB * k + SB], SB * k, 1), rhs)
-        p2s[rd, 0:SB] = rhs
-        p2s[rd, SB : SB + 8] = dots
+        p2s[rd] = rhs
         p2r[rd, row] = p2s[rd]
         along_row(p2s.at[rd], p2r.at[rd, row], s2.at[rd], r2.at[rd])
 
-    def sum_tiles(buf, at):
-        total = buf[0, at : at + 8]
+    def sum_tiles(buf):
+        total = buf[0]
         for i in range(1, N):
-            total = total + buf[i, at : at + 8]
+            total = total + buf[i]
         return total
+
+    def dots_row(rd, dots):
+        d2s[rd] = dots
+        d2r[rd, row] = dots
+        along_row(d2s.at[rd], d2r.at[rd, row], s4.at[rd], r4.at[rd])
+
+    def dots_col(rd):
+        wait_many(d2r.at[rd], r4.at[rd])
+        dots = sum_tiles(d2r.at[rd])
+        d3s[rd] = dots
+        d3r[rd, col] = dots
+        along_col(1, 0, lambda to: d3s.at[rd], d3r.at[rd, col], s5.at[rd], r5.at[rd])
+
+    def dots_total(rd):
+        wait_many(d3r.at[rd], r5.at[rd])
+        return sum_tiles(d3r.at[rd])
 
     def solve(rd):
         wait_many(p2r.at[rd], r2.at[rd])
-        rhs = jnp.concatenate([p2r[rd, i, 0:SB] for i in range(N)], axis=1)
+        rhs = jnp.concatenate([p2r[rd, i] for i in range(N)], axis=1)
         hi, lo = split(rhs)
         both = mm_nt(jnp.concatenate([hi, lo], axis=0), chi[...])
         solved = both[0:SB] + (both[SB : 2 * SB] + mm_nt(hi, clo[...]))
         pieces = [solved] + [pltpu.roll(solved, 128 - SB * k, 1) for k in range(1, K)]
         own = jnp.concatenate(pieces, axis=0).T[0:N]
         east_of, west_of = up_one(own), down_one(own)
-        dots = sum_tiles(p2r.at[rd], SB)
         p3ns[rd] = own.reshape(N, 1, 128)
         for i in range(N):
-            p3s[rd, i, 0:8] = rows_tile([part[i : i + 1] for part in (own, west_of, east_of)])
-            p3s[rd, i, 8:16] = dots
+            p3s[rd, i] = rows_tile([part[i : i + 1] for part in (own, west_of, east_of)])
         p3r[rd, col] = p3s[rd, col]
         three_rows(
             p3ns.at[rd], p3ns.at[rd], p3nr.at[rd, 1], p3nr.at[rd, 0], lambda to: p3s.at[rd, to], p3r.at[rd, col],
@@ -318,7 +332,7 @@
         three_waits(p3r.at[rd], p3nr.at[rd], r3.at[rd])
         own, west_of, east_of = [jnp.concatenate([p3r[rd, i, g : g + 1] for i in range(N)], axis=0) for g in range(3)]
         parts = [own, p3nr[rd, 0].reshape(N, 128), p3nr[rd, 1].reshape(N, 128), west_of, east_of]
-        return jnp.concatenate([from_blocks(part) for part in parts], axis=0), sum_tiles(p3r.at[rd], 8)
+        return jnp.concatenate([from_blocks(part) for part in parts], axis=0)
 
     def set_tau(new):
         tau[...] = new
@@ -401,7 +415,7 @@
     get_s.wait()
     prepare_rows(0)
     prepare_rows(1)
-    gather_rows(0, jnp.zeros((8, 128), f32), lambda: chunk(0, 2))
+    gather_rows(0, lambda: chunk(0, 2))
     pass_cinv()
     chunk(0, 3)
     prepare_rows(2)
@@ -427,7 +441,7 @@
     pad = jnp.zeros((16, NI), f32)
     bcat[...] = jnp.concatenate([bhi32, pad, bhi32, pad, blo32, pad, jnp.zeros((64, NI), f32)], axis=0).T.astype(bf16)
     dcol[...] = jnp.broadcast_to(jnp.concatenate(drow, axis=1), (128, NI)).T
-    set_tau(solutions(0)[0])
+    set_tau(solutions(0))
     gamma = jnp.zeros((1, SC), f32)
     for f in (3, 2, 1, 0):
         at = slice(f * F, (f + 1) * F)
@@ -443,31 +457,24 @@
         if not last:
             contributions(rd, gst)
         delta = apply_schur(rd, (lambda f: None) if last else (lambda f: chunk(rd, 0, (f,))))
-        dots = dot_tile(delta, gamma, eps)
+        dots_row(rd, dot_tile(delta, gamma, eps))
         if not last:
             if pending is not None:
                 move(*pending, None)
-            gather_rows(rd, dots, lambda: chunk(rd, 1))
+            gather_rows(rd, lambda: chunk(rd, 1))
             chunk(rd, 2)
+            dots_col(rd)
             solve(rd)
             chunk(rd, 3)
-            solved, total = solutions(rd)
+            solved = solutions(rd)
         else:
-            p2s[rd, SB : SB + 8] = dots
-            p2r[rd, row, SB : SB + 8] = dots
-            along_row(p2s.at[rd, pl.ds(SB, 8)], p2r.at[rd, row, pl.ds(SB, 8)], s2.at[rd], r2.at[rd])
             chunk(rd, 0)
             chunk(rd, 1)
             chunk(rd, 2)
             move(*pending, None)
-            wait_many(p2r.at[rd, :, pl.ds(SB, 8)], r2.at[rd])
-            dots = sum_tiles(p2r.at[rd], SB)
-            p3s[rd, 0, 8:16] = dots
-            p3r[rd, col, 8:16] = dots
-            along_col(1, 0, lambda to: p3s.at[rd, 0, pl.ds(8, 8)], p3r.at[rd, col, pl.ds(8, 8)], s3.at[rd, 0], r3.at[rd, 0])
+            dots_col(rd)
             chunk(rd, 3)
-            wait_many(p3r.at[rd, :, pl.ds(8, 8)], r3.at[rd, 0])
-            total = sum_tiles(p3r.at[rd], 8)
+        total = dots_total(rd)
         delta_t, gamma_t, eps_t = scalars(total)
         if rd == 1:
             beta = None
@@ -520,9 +527,30 @@
             three_waits(p1r.at[rd], p1nr.at[rd], s1.at[rd])
             wait_many(p2r.at[rd], s2.at[rd])
             three_waits(p3r.at[rd], p3nr.at[rd], s3.at[rd])
-        else:
-            wait_many(p2r.at[rd, :, pl.ds(SB, 8)], s2.at[rd])
-            wait_many(p3r.at[rd, :, pl.ds(8, 8)], s3.at[rd, 0])
+        if rd > 0:
+            wait_many(d2r.at[rd], s4.at[rd])
+            wait_many(d3r.at[rd], s5.at[rd])
+
+
+def deliver(a, b, a_out, b_out, a_mid, b_mid, in_sem, out_sem):
+    rows = NI // PIECES
+    pieces = [(i, j) for i in range(PIECES) for j in range(2)]
+
+    def inward(i, j):
+        at = pl.ds(i * rows, rows)
+        return pltpu.make_async_copy((a, b)[j].at[at], (a_mid, b_mid)[j].at[at], in_sem.at[j, i])
+
+    def outward(i, j):
+        at = pl.ds(i * rows, rows)
+        return pltpu.make_async_copy((a_mid, b_mid)[j].at[at], (a_out, b_out)[j].at[at], out_sem.at[j, i])
+
+    for piece in pieces:
+        inward(*piece).start()
+    for piece in pieces:
+        inward(*piece).wait()
+        outward(*piece).start()
+    for piece in pieces:
+        outward(*piece).wait()
 
 
 def body(schur, load, dscale, basis, coarse_inv, north_match, west_match):
@@ -550,17 +578,26 @@
             buf(N, K, N * 128), buf(128, N * 128, dtype=bf16), buf(128, N * 128, dtype=bf16),
             buf(ROUNDS, 4, F, SC),
             buf(ROUNDS, N, 8, 128), buf(ROUNDS, N, 8, 128), buf(ROUNDS, 2, N, 1, 128), buf(ROUNDS, 2, N, 1, 128),
-            buf(ROUNDS, SB + 8, 128), buf(ROUNDS, N, SB + 8, 128),
-            buf(ROUNDS, N, 16, 128), buf(ROUNDS, N, 16, 128), buf(ROUNDS, N, 1, 128), buf(ROUNDS, 2, N, 1, 128),
+            buf(ROUNDS, SB, 128), buf(ROUNDS, N, SB, 128),
+            buf(ROUNDS, N, 8, 128), buf(ROUNDS, N, 8, 128), buf(ROUNDS, N, 1, 128), buf(ROUNDS, 2, N, 1, 128),
             buf(128, 128, dtype=bf16),
+            buf(ROUNDS, 8, 128), buf(ROUNDS, N, 8, 128), buf(ROUNDS, 8, 128), buf(ROUNDS, N, 8, 128),
             dma((7,)), dma((ROUNDS, 4)), dma((ROUNDS, 4)), dma((4,)), dma((4,)), dma((2,)), dma((2,)),
             dma((ROUNDS, 3)), dma((ROUNDS, 3)), dma((ROUNDS,)), dma((ROUNDS,)), dma((ROUNDS, 3)), dma((ROUNDS, 3)), dma((2,)),
+            dma((ROUNDS,)), dma((ROUNDS,)), dma((ROUNDS,)), dma((ROUNDS,)),
         ],
         compiler_params=pltpu.CompilerParams(collective_id=0, has_side_effects=True, vmem_limit_bytes=63 << 20),
     )(
         schur.reshape(NI, NI), load.reshape(NI, SC), dscale.reshape(1, NI), basis.reshape(K, NI),
         coarse_inv, north_match.reshape(1, F), west_match.reshape(1, F),
     )
+    solved, left = pl.pallas_call(
+        deliver,
+        out_shape=[jax.ShapeDtypeStruct((NI, SC), f32)] * 2,
+        in_specs=[hbm] * 2,
+        out_specs=[hbm] * 2,
+        scratch_shapes=[vec, vec, dma((2, PIECES)), dma((2, PIECES))],
+    )(solved, left)
     return solved.reshape(1, 1, NI, SC), left.reshape(1, 1, NI, SC)
 
 

time: 123 us -> 120 us (0.976)
  local copies, waits for them, and re-layouts: 4.52 us -> 0 us
    unnamed x2 -> x0, local copies, waits for them, and re-layouts: 4.52 us -> none
    pallas_call x0 -> x1, Pallas kernels: none -> 2.39 us  [body(): pl.pallas_call(deliver, out_shape=[jax.ShapeDtypeStruct((NI, SC), f32)] *...]
where the time goes in v4:
time: 120 us
  Pallas kernels  119 us (99%)
    pallas_call x1, Pallas kernels, body(): pl.pallas_call(kernel, out_shape=[jax.ShapeDtypeStruct((NI, SC), f32)] *...  117 us

profile of v4, /device:TPU:1, one launch (start us, length us, event | category | flops | bytes accessed | tf_op | source)
XLA Modules:
  0.0 120.1 jit_solution(15709167579036235135)
XLA Ops:
  0.6 116.9 %shard_map.86 = (f32[1024,256]{1,0:T(8,128)}, f32[1024,256]{1,0:T(8,128)}) custom-call(f32[1024,1024]{1,0:T(8,128)} %bitcast.8, f32[1024,256]{1,0:T(8,128)} %bitcast.9, f32[1,1024]{1,0:T(1,128)} %bitcast.11, f32[8,1024]{1,0:T(8,128)} %bitcast.10, f32[8,2048]{1,0:T(8,128)} %cinv_in.1, s32[1,256]{1,0:T(1,128)} %bitcast.12, s32[1,256]{1,0:T(1,128)} %bitcast.13), custom_call_target="tpu_custom_call" | custom-call | tf_op jit(solution)/shard_map/pallas_call | solution.py:566
  117.5 2.4 %shard_map.87 = (f32[1024,256]{1,0:T(8,128)}, f32[1024,256]{1,0:T(8,128)}) custom-call(f32[1024,256]{1,0:T(8,128)} %get-tuple-element.6.a, f32[1024,256]{1,0:T(8,128)} %get-tuple-element.7.b), custom_call_target="tpu_custom_call" | custom-call | tf_op jit(solution)/shard_map/pallas_call | solution.py:594

commit v5 on v4

--- a/solution.py
+++ b/solution.py
@@ -456,7 +456,7 @@
         last = rd == ROUNDS - 1
         if not last:
             contributions(rd, gst)
-        delta = apply_schur(rd, (lambda f: None) if last else (lambda f: chunk(rd, 0, (f,))))
+        delta = apply_schur(rd, lambda f: chunk(rd, 0, (f,)))
         dots_row(rd, dot_tile(delta, gamma, eps))
         if not last:
             if pending is not None:
@@ -468,7 +468,6 @@
             chunk(rd, 3)
             solved = solutions(rd)
         else:
-            chunk(rd, 0)
             chunk(rd, 1)
             chunk(rd, 2)
             move(*pending, None)

time: 120 us -> 120 us (level)
  no operation moved by 1% of the time
where the time goes in v5:
time: 120 us
  Pallas kernels  119 us (99%)
    pallas_call x1, Pallas kernels, body(): pl.pallas_call(kernel, out_shape=[jax.ShapeDtypeStruct((NI, SC), f32)] *...  116 us

profile of v5, /device:TPU:1, one launch (start us, length us, event | category | flops | bytes accessed | tf_op | source)
XLA Modules:
  0.0 119.6 jit_solution(2422874493565726545)
XLA Ops:
  0.6 116.4 %shard_map.86 = (f32[1024,256]{1,0:T(8,128)}, f32[1024,256]{1,0:T(8,128)}) custom-call(f32[1024,1024]{1,0:T(8,128)} %bitcast.8, f32[1024,256]{1,0:T(8,128)} %bitcast.9, f32[1,1024]{1,0:T(1,128)} %bitcast.11, f32[8,1024]{1,0:T(8,128)} %bitcast.10, f32[8,2048]{1,0:T(8,128)} %cinv_in.1, s32[1,256]{1,0:T(1,128)} %bitcast.12, s32[1,256]{1,0:T(1,128)} %bitcast.13), custom_call_target="tpu_custom_call" | custom-call | tf_op jit(solution)/shard_map/pallas_call | solution.py:565
  117.1 2.4 %shard_map.87 = (f32[1024,256]{1,0:T(8,128)}, f32[1024,256]{1,0:T(8,128)}) custom-call(f32[1024,256]{1,0:T(8,128)} %get-tuple-element.6.a, f32[1024,256]{1,0:T(8,128)} %get-tuple-element.7.b), custom_call_target="tpu_custom_call" | custom-call | tf_op jit(solution)/shard_map/pallas_call | solution.py:593
